TPU v7x, 32 devices: a whole 2x2x4 slice. The times are simulated.
32 devices in a mesh: dp: 8 (over y, x, core), seq: 4 (over z).
Axes of the slice: x: 2, y: 2, z: 4, core: 2. Of those that a mesh axis runs over, the one named last changes fastest.
Arguments:
- tokens: bfloat16 [32, 512, 768], P('dp', 'seq'), may hold values from -6 to 6
- segment_ids: int32 [32, 512], P('dp', 'seq'), may hold values from 0 to 7, as said below
- pair_ids: int32 [256], P('dp'), may hold values from 0 to 31
- w_qkv: bfloat16 [2, 768, 2304], replicated, may hold values from -0.21875 to 0.21875
- b_query: float32 [2, 768], replicated, may hold values from -3 to 3
- b_value: float32 [2, 768], replicated, may hold values from -3 to 3
- w_out: bfloat16 [2, 768, 768], replicated, may hold values from -0.625 to 0.625
- b_out: float32 [2, 768], replicated, may hold values from -3 to 3
- gain_one: float32 [2, 768], replicated, may hold values from 0.1 to 1.9
- shift_one: float32 [2, 768], replicated, may hold values from -3 to 3
- w_up: bfloat16 [2, 768, 3072], replicated, may hold values from -0.21875 to 0.21875
- b_up: float32 [2, 3072], replicated, may hold values from -3 to 3
- w_down: bfloat16 [2, 3072, 768], replicated, may hold values from -0.109375 to 0.109375
- b_down: float32 [2, 768], replicated, may hold values from -3 to 3
- gain_two: float32 [2, 768], replicated, may hold values from 0.1 to 1.9
- shift_two: float32 [2, 768], replicated, may hold values from -3 to 3
Outputs:
- loss: float32 [8], P('dp')
- grad_tokens: float32 [32, 512, 768], P('dp', 'seq')
- grad_w_qkv: float32 [2, 768, 2304], P(None, 'dp')
- grad_b_query: float32 [2, 768], replicated
- grad_b_value: float32 [2, 768], replicated
- grad_w_out: float32 [2, 768, 768], P(None, 'dp')
- grad_b_out: float32 [2, 768], replicated
- grad_gain_one: float32 [2, 768], replicated
- grad_shift_one: float32 [2, 768], replicated
- grad_w_up: float32 [2, 768, 3072], P(None, 'dp')
- grad_b_up: float32 [2, 3072], replicated
- grad_w_down: float32 [2, 3072, 768], P(None, 'dp')
- grad_b_down: float32 [2, 768], replicated
- grad_gain_two: float32 [2, 768], replicated
- grad_shift_two: float32 [2, 768], replicated
Inputs may be any that keep to these rules, and one draw needn't show every extreme that they name: `segment_ids`: each row holds exactly 8 segments, numbered 0 to 7 in order of position, each of one or more tokens. The partner of segment i of index g of dp is the segment of number pair_ids[i] among the 32 segments of the same g.
All inputs are finite; a program needn't handle non-finite values.
Results may differ from a plain program's by a relative error of at most 0.02.
Values may be sent and summed in bfloat16 or wider, within the bound.
A program may use at most 256 MiB of HBM per device.

v0:
```python
import jax
import jax.numpy as jnp
from jax import lax
from jax.sharding import PartitionSpec as P

HD = 64


highest = lax.Precision.HIGHEST
norm_eps = 1e-06
loss_scale = 1024.0


def exact_gelu(values):
    return jax.nn.gelu(values, approximate=False)


def outer_sum(left, right):
    return lax.dot_general(
        left, right, (((0,), (0,)), ((), ())), preferred_element_type=jnp.float32
    )


def times_transpose(left, right):
    return lax.dot_general(
        left, right, (((1,), (1,)), ((), ())), preferred_element_type=jnp.float32
    )


def norm_forward(values, gain_vec, shift_vec):
    centre = values - jnp.mean(values, axis=-1, keepdims=True)
    scaled = lax.rsqrt(jnp.mean(centre * centre, axis=-1, keepdims=True) + norm_eps)
    normal = centre * scaled
    return (normal * gain_vec + shift_vec, normal, scaled)


def norm_backward(grad_out, normal, scaled, gain_vec):
    grad_normal = grad_out * gain_vec
    grad_in = scaled * (
        grad_normal
        - jnp.mean(grad_normal, axis=-1, keepdims=True)
        - normal * jnp.mean(grad_normal * normal, axis=-1, keepdims=True)
    )
    return (grad_in, jnp.sum(grad_out * normal, axis=0), jnp.sum(grad_out, axis=0))


def score_block(queries, keys_all, seg_local, seg_all):
    row_count = seg_local.shape[0]
    head_count = queries.shape[-1] // HD
    query_heads = queries.reshape(row_count, -1, head_count, HD)
    key_heads = keys_all.reshape(row_count, -1, head_count, HD)
    raw = (
        jnp.einsum("rqhd,rkhd->rhqk", query_heads, key_heads, preferred_element_type=jnp.float32)
        * 0.125
    )
    allowed = (seg_local[:, :, None] == seg_all[:, None, :])[:, None]
    return (jnp.where(allowed, raw, -1e30), query_heads, key_heads)


def attention_forward(queries, gathered, seg_local):
    keys_all, values_all, seg_all = gathered
    row_count = seg_local.shape[0]
    masked, query_heads, key_heads = score_block(queries, keys_all, seg_local, seg_all)
    top_score = jnp.max(masked, axis=-1, keepdims=True)
    log_total = top_score + jnp.log(jnp.sum(jnp.exp(masked - top_score), axis=-1, keepdims=True))
    probs_low = jnp.exp(masked - log_total).astype(jnp.bfloat16)
    value_heads = values_all.reshape(row_count, -1, key_heads.shape[2], HD)
    mixed = jnp.einsum(
        "rhqk,rkhd->rqhd", probs_low, value_heads, preferred_element_type=jnp.float32
    )
    return (log_total, mixed.reshape(queries.shape[0], -1))


def attention_backward(queries, gathered, seg_local, log_total, grad_mixed):
    keys_all, values_all, seg_all = gathered
    row_count = seg_local.shape[0]
    masked, query_heads, key_heads = score_block(queries, keys_all, seg_local, seg_all)
    probs = jnp.exp(masked - log_total)
    value_heads = values_all.reshape(row_count, -1, key_heads.shape[2], HD)
    grad_heads = grad_mixed.reshape(query_heads.shape)
    grad_probs = jnp.einsum(
        "rqhd,rkhd->rhqk", grad_heads, value_heads, preferred_element_type=jnp.float32
    )
    inner = jnp.sum(probs * grad_probs, axis=-1, keepdims=True)
    grad_scores = (probs * (grad_probs - inner)).astype(jnp.bfloat16)
    grad_query = (
        jnp.einsum("rhqk,rkhd->rqhd", grad_scores, key_heads, preferred_element_type=jnp.float32)
        * 0.125
    )
    grad_keys_all = (
        jnp.einsum("rhqk,rqhd->rkhd", grad_scores, query_heads, preferred_element_type=jnp.float32)
        * 0.125
    )
    grad_values_all = jnp.einsum(
        "rhqk,rqhd->rkhd",
        probs.astype(jnp.bfloat16),
        grad_heads,
        preferred_element_type=jnp.float32,
    )
    model_width = queries.shape[-1]
    return (
        grad_query.reshape(queries.shape[0], model_width),
        grad_keys_all.reshape(row_count, -1, model_width),
        grad_values_all.reshape(row_count, -1, model_width),
    )


def layer_forward(hidden, hidden_low, seg_local, weights):
    (
        w_qkv,
        b_query,
        b_value,
        w_out,
        b_out,
        gain_one,
        shift_one,
        w_up,
        b_up,
        w_down,
        b_down,
        gain_two,
        shift_two,
    ) = weights
    row_count = seg_local.shape[0]
    model_width = w_out.shape[0]
    bias_all = jnp.concatenate([b_query, jnp.zeros_like(b_query), b_value])
    projected = (jnp.dot(hidden_low, w_qkv, preferred_element_type=jnp.float32) + bias_all).astype(
        jnp.bfloat16
    )
    queries = projected[:, :model_width]
    keys_local = projected[:, model_width : 2 * model_width].reshape(row_count, -1, model_width)
    values_local = projected[:, 2 * model_width :].reshape(row_count, -1, model_width)
    gathered = (
        lax.all_gather(keys_local, "seq", axis=1, tiled=True),
        lax.all_gather(values_local, "seq", axis=1, tiled=True),
        lax.all_gather(seg_local, "seq", axis=1, tiled=True),
    )
    log_total, mixed = attention_forward(queries, gathered, seg_local)
    mixed_low = mixed.astype(jnp.bfloat16)
    branch = jnp.dot(mixed_low, w_out, preferred_element_type=jnp.float32) + b_out
    normed, normal_one, scaled_one = norm_forward(hidden + branch, gain_one, shift_one)
    normed_low = normed.astype(jnp.bfloat16)
    pre_act = jnp.dot(normed_low, w_up, preferred_element_type=jnp.float32) + b_up
    activated_low = exact_gelu(pre_act).astype(jnp.bfloat16)
    second = jnp.dot(activated_low, w_down, preferred_element_type=jnp.float32) + b_down
    result, normal_two, scaled_two = norm_forward(normed + second, gain_two, shift_two)
    kept_state = (
        hidden_low,
        queries,
        keys_local,
        values_local,
        gathered,
        log_total,
        mixed_low,
        normal_one,
        scaled_one,
        normed_low,
        pre_act,
        activated_low,
        normal_two,
        scaled_two,
    )
    return (result, kept_state)


def layer_backward(grad_out, kept_state, weights, seg_local):
    (
        w_qkv,
        b_query,
        b_value,
        w_out,
        b_out,
        gain_one,
        shift_one,
        w_up,
        b_up,
        w_down,
        b_down,
        gain_two,
        shift_two,
    ) = weights
    (
        hidden_low,
        queries,
        keys_local,
        values_local,
        gathered,
        log_total,
        mixed_low,
        normal_one,
        scaled_one,
        normed_low,
        pre_act,
        activated_low,
        normal_two,
        scaled_two,
    ) = kept_state
    model_width = w_out.shape[0]
    grad_sum_two, grad_gain_two, grad_shift_two = norm_backward(
        grad_out, normal_two, scaled_two, gain_two
    )
    grad_second = grad_sum_two.astype(jnp.bfloat16)
    grad_w_down = outer_sum(activated_low, grad_second)
    grad_b_down = jnp.sum(grad_second.astype(jnp.float32), axis=0)
    grad_act = times_transpose(grad_second, w_down)
    gelu_pull = jax.vjp(exact_gelu, pre_act)[1]
    grad_pre = gelu_pull(grad_act)[0].astype(jnp.bfloat16)
    grad_w_up = outer_sum(normed_low, grad_pre)
    grad_b_up = jnp.sum(grad_pre.astype(jnp.float32), axis=0)
    grad_normed = grad_sum_two + times_transpose(grad_pre, w_up)
    grad_sum_one, grad_gain_one, grad_shift_one = norm_backward(
        grad_normed, normal_one, scaled_one, gain_one
    )
    grad_branch = grad_sum_one.astype(jnp.bfloat16)
    grad_w_out = outer_sum(mixed_low, grad_branch)
    grad_b_out = jnp.sum(grad_branch.astype(jnp.float32), axis=0)
    grad_mixed = times_transpose(grad_branch, w_out).astype(jnp.bfloat16)
    grad_query, grad_keys_all, grad_values_all = attention_backward(
        queries, gathered, seg_local, log_total, grad_mixed
    )
    grad_keys, grad_values = (
        lax.psum_scatter(
            grad_keys_all.astype(jnp.bfloat16), "seq", scatter_dimension=1, tiled=True
        ).astype(jnp.float32),
        lax.psum_scatter(
            grad_values_all.astype(jnp.bfloat16), "seq", scatter_dimension=1, tiled=True
        ).astype(jnp.float32),
    )
    grad_projected = jnp.concatenate(
        [grad_query, grad_keys.reshape(-1, model_width), grad_values.reshape(-1, model_width)],
        axis=-1,
    ).astype(jnp.bfloat16)
    grad_w_qkv = outer_sum(hidden_low, grad_projected)
    bias_sums = jnp.sum(grad_projected.astype(jnp.float32), axis=0)
    grad_b_query = bias_sums[:model_width]
    grad_b_value = bias_sums[2 * model_width :]
    grad_input = grad_sum_one + times_transpose(grad_projected, w_qkv)
    layer_grads = (
        grad_w_qkv,
        grad_b_query,
        grad_b_value,
        grad_w_out,
        grad_b_out,
        grad_gain_one,
        grad_shift_one,
        grad_w_up,
        grad_b_up,
        grad_w_down,
        grad_b_down,
        grad_gain_two,
        grad_shift_two,
    )
    return (grad_input, layer_grads)


def pooled_loss(pooled_sums, counts, pair_local):
    embed = pooled_sums / counts[:, None]
    unit = embed * lax.rsqrt(jnp.sum(embed * embed, axis=-1, keepdims=True) + norm_eps)
    logits = 20.0 * jnp.dot(unit, unit.T, precision=highest)
    chosen = pair_local[:, None] == jnp.arange(pair_local.shape[0], dtype=jnp.int32)[None, :]
    picked = jnp.sum(jnp.where(chosen, logits, 0.0), axis=-1)
    return jnp.mean(jax.nn.logsumexp(logits, axis=-1) - picked)


def on_device(
    tokens,
    segment_ids,
    pair_ids,
    w_qkv,
    b_query,
    b_value,
    w_out,
    b_out,
    gain_one,
    shift_one,
    w_up,
    b_up,
    w_down,
    b_down,
    gain_two,
    shift_two,
):
    shard_shape = tokens.shape
    seg_count = pair_ids.shape[0]
    segs_row = seg_count // shard_shape[0]
    row_count = tokens.shape[0]
    model_width = tokens.shape[2]
    hidden_low = tokens.reshape(-1, model_width)
    hidden = hidden_low.astype(jnp.float32)
    all_weights = (
        w_qkv,
        b_query,
        b_value,
        w_out,
        b_out,
        gain_one,
        shift_one,
        w_up,
        b_up,
        w_down,
        b_down,
        gain_two,
        shift_two,
    )
    layer_count = w_qkv.shape[0]
    states = []
    for layer_index in range(layer_count):
        weights = tuple((stacked[layer_index] for stacked in all_weights))
        hidden, kept_state = layer_forward(hidden, hidden_low, segment_ids, weights)
        states.append(kept_state)
        hidden_low = hidden.astype(jnp.bfloat16)
    row_numbers = jnp.arange(row_count, dtype=jnp.int32)
    global_ids = segment_ids + segs_row * row_numbers[:, None]
    member = (
        global_ids.reshape(-1)[:, None] == jnp.arange(seg_count, dtype=jnp.int32)[None, :]
    ).astype(jnp.float32)
    pooled_sums = jnp.einsum("ts,td->sd", member, hidden, precision=highest)
    counts = jnp.sum(member, axis=0)
    pooled_sums, counts = (
        lax.psum(pooled_sums.astype(jnp.bfloat16), "seq").astype(jnp.float32),
        lax.psum(counts.astype(jnp.bfloat16), "seq").astype(jnp.float32),
    )
    loss_value, pullback = jax.vjp(
        lambda sums_in: pooled_loss(sums_in, counts, pair_ids), pooled_sums
    )
    grad_sums = pullback(jnp.float32(loss_scale))[0]
    grad_hidden = jnp.einsum("ts,sd->td", member, grad_sums, precision=highest)
    grads_all = [None] * layer_count
    for layer_index in reversed(range(layer_count)):
        weights = tuple((stacked[layer_index] for stacked in all_weights))
        grad_hidden, grads_all[layer_index] = layer_backward(
            grad_hidden, states[layer_index], weights, segment_ids
        )
    grad_tokens = grad_hidden.reshape(tokens.shape)
    stacked_grads = tuple(
        (
            jnp.stack([layer_grads[member_index] for layer_grads in grads_all])
            for member_index in range(13)
        )
    )
    matrices = (stacked_grads[0], stacked_grads[3], stacked_grads[7], stacked_grads[9])
    vectors = (
        stacked_grads[1],
        stacked_grads[2],
        stacked_grads[4],
        stacked_grads[5],
        stacked_grads[6],
        stacked_grads[8],
        stacked_grads[10],
        stacked_grads[11],
        stacked_grads[12],
    )
    matrices = (
        lax.psum_scatter(matrices[0], "dp", scatter_dimension=1, tiled=True),
        lax.psum_scatter(matrices[1], "dp", scatter_dimension=1, tiled=True),
        lax.psum_scatter(matrices[2], "dp", scatter_dimension=1, tiled=True),
        lax.psum_scatter(matrices[3], "dp", scatter_dimension=1, tiled=True),
    )
    matrices = (
        lax.psum_scatter(
            matrices[0].astype(jnp.bfloat16), "seq", scatter_dimension=2, tiled=True
        ).astype(jnp.float32),
        lax.psum_scatter(
            matrices[1].astype(jnp.bfloat16), "seq", scatter_dimension=2, tiled=True
        ).astype(jnp.float32),
        lax.psum_scatter(
            matrices[2].astype(jnp.bfloat16), "seq", scatter_dimension=2, tiled=True
        ).astype(jnp.float32),
        lax.psum_scatter(
            matrices[3].astype(jnp.bfloat16), "seq", scatter_dimension=2, tiled=True
        ).astype(jnp.float32),
    )
    matrices = (
        lax.all_gather(matrices[0].astype(jnp.bfloat16), "seq", axis=2, tiled=True).astype(
            jnp.float32
        ),
        lax.all_gather(matrices[1].astype(jnp.bfloat16), "seq", axis=2, tiled=True).astype(
            jnp.float32
        ),
        lax.all_gather(matrices[2].astype(jnp.bfloat16), "seq", axis=2, tiled=True).astype(
            jnp.float32
        ),
        lax.all_gather(matrices[3].astype(jnp.bfloat16), "seq", axis=2, tiled=True).astype(
            jnp.float32
        ),
    )
    vectors = lax.psum(
        (
            vectors[0],
            vectors[1],
            vectors[2],
            vectors[3],
            vectors[4],
            vectors[5],
            vectors[6],
            vectors[7],
            vectors[8],
        ),
        ("dp", "seq"),
    )
    return (
        loss_value.reshape(1),
        grad_tokens,
        matrices[0],
        vectors[0],
        vectors[1],
        matrices[1],
        vectors[2],
        vectors[3],
        vectors[4],
        matrices[2],
        vectors[5],
        matrices[3],
        vectors[6],
        vectors[7],
        vectors[8],
    )


def solution(mesh):
    return jax.shard_map(
        on_device,
        mesh=mesh,
        in_specs=(
            P("dp", "seq", None),
            P("dp", "seq"),
            P("dp"),
            P(),
            P(),
            P(),
            P(),
            P(),
            P(),
            P(),
            P(),
            P(),
            P(),
            P(),
            P(),
            P(),
        ),
        out_specs=(
            P("dp"),
            P("dp", "seq", None),
            P(None, "dp", None),
            P(),
            P(),
            P(None, "dp", None),
            P(),
            P(),
            P(),
            P(None, "dp", None),
            P(),
            P(None, "dp", None),
            P(),
            P(),
            P(),
        ),
        check_vma=False,
    )
```

profile of v0, /device:TPU:0, one launch (start us, length us, event | category | flops | bytes accessed | tf_op | source)
XLA Modules:
  0.0 1673.8 jit_solution(255930367567267716)
XLA Ops:
  15.9 13.6 all_gather.29
  31.2 48.8 %all-gather.9.cloned.1.call-done = bf16[4,512,768]{2,1,0:T(8,128)(2,1)} async-done(((bf16[4,128,768]{2,1,0:T(8,128)(2,1)}), bf16[4,512,768]{2,1,0:T(8,128)(2,1)}) %all-gather.9.cloned.1.call-update) | async-done | bytes 3145744 | tf_op jit(solution)/shard_map/all_gather | solution.py:134
  92.3 52.1 %all-gather.7.cloned.1.call-done = bf16[4,512,768]{2,1,0:T(8,128)(2,1)} async-done(((bf16[4,128,768]{2,1,0:T(8,128)(2,1)}), bf16[4,512,768]{2,1,0:T(8,128)(2,1)}) %all-gather.7.cloned.1.call-update) | async-done | bytes 3145744 | tf_op jit(solution)/shard_map/all_gather | solution.py:135
  147.7 7.6 fusion.78
  157.3 19.2 %multiply_convert_fusion.5 = (bf16[512,3072]{1,0:T(8,128)(2,1)S(1)}, f32[512,3072]{1,0:T(8,128)}, f32[512,3072]{1,0:T(8,128)}) fusion(f32[3072]{0:T(1024)S(1)} %bitcast.249, bf16[2,768,3072]{2,1,0:T(8,128)(2,1)S(1)} %bitcast.259, f32[512,768]{1,0:T(8,128)S(1)} %get-tuple-element.166, f32[768]{0:T(1024)S(1)} %get-tuple-element.117, ...), kind=kOutput, calls=%fused_computation.40 | convolution fusion | flops 2521694208 | bytes 22044672 | tf_op jit(solution)/shard_map/dot_general | solution.py:143
  185.9 59.6 %all-gather.13.cloned.1.call-done = bf16[4,512,768]{2,1,0:T(8,128)(2,1)} async-done(((bf16[4,128,768]{2,1,0:T(8,128)(2,1)}), bf16[4,512,768]{2,1,0:T(8,128)(2,1)}) %all-gather.13.cloned.1.call-update) | async-done | bytes 3145744 | tf_op jit(solution)/shard_map/all_gather | solution.py:134
  257.3 52.3 %all-gather.11.cloned.1.call-done = bf16[4,512,768]{2,1,0:T(8,128)(2,1)} async-done(((bf16[4,128,768]{2,1,0:T(8,128)(2,1)}), bf16[4,512,768]{2,1,0:T(8,128)(2,1)}) %all-gather.11.cloned.1.call-update) | async-done | bytes 3145744 | tf_op jit(solution)/shard_map/all_gather | solution.py:135
  314.3 9.0 fusion.79
  325.6 21.1 %multiply_convert_fusion.4 = (bf16[512,3072]{1,0:T(8,128)(2,1)S(1)}, f32[512,3072]{1,0:T(8,128)}, f32[512,3072]{1,0:T(8,128)}) fusion(f32[3072]{0:T(1024)S(1)} %bitcast.252, bf16[2,768,3072]{2,1,0:T(8,128)(2,1)} %param.26, f32[512,768]{1,0:T(8,128)S(1)} %get-tuple-element.173, f32[768]{0:T(1024)S(1)} %get-tuple-element.116, ...), kind=kOutput, calls=%fused_computation.27 | convolution fusion | flops 2521694208 | bytes 22042624 | tf_op jit(solution)/shard_map/dot_general | solution.py:143
  351.6 18.4 %all-reduce.3 = (bf16[32]{0:T(256)(128)(2,1)}, bf16[32,768]{1,0:T(8,128)(2,1)S(1)}) all-reduce(bf16[32]{0:T(256)(128)(2,1)} %convert_reduce_fusion.8, bf16[32,768]{1,0:T(8,128)(2,1)S(1)} %fusion.86), channel_id=1, replica_groups=mesh['dp'=8,'seq'=4] {'seq'}, use_global_device_ids=true, to_apply=%region_14.15 | all-reduce | flops 24608 | bytes 98432 | tf_op jit(solution)/shard_map/psum | solution.py:321
  380.0 8.8 convert_reduce_fusion
  401.2 8.6 multiply_reduce_fusion.1
  409.8 7.2 multiply_convert_fusion.1
  425.3 9.7 convolution_convert_fusion.1
  439.8 5.2 fusion.80
  446.7 5.4 convolution_bitcast_fusion.2
  452.1 32.0 %reduce-scatter.15.cloned.1.call-done = bf16[4,128,768]{2,1,0:T(8,128)(2,1)} async-done(((bf16[4,512,768]{2,1,0:T(8,128)(2,1)}), bf16[4,128,768]{2,1,0:T(8,128)(2,1)}) %reduce-scatter.15.cloned.1.call-update) | async-done | bytes 786448 | tf_op jit(solution)/shard_map/reduce_scatter | solution.py:222
  486.4 60.2 %reduce-scatter.17.cloned.1.call-done = bf16[4,128,768]{2,1,0:T(8,128)(2,1)} async-done(((bf16[4,512,768]{2,1,0:T(8,128)(2,1)}), bf16[4,128,768]{2,1,0:T(8,128)(2,1)}) %reduce-scatter.17.cloned.1.call-update) | async-done | bytes 786448 | tf_op jit(solution)/shard_map/reduce_scatter | solution.py:225
  548.9 6.1 multiply_reduce_fusion.3
  559.7 6.7 pad_maximum_fusion.1
  572.6 11.9 convert_reduce_fusion.1
  587.5 9.2 pad_maximum_fusion
  596.8 6.5 multiply_reduce_fusion.5
  612.5 8.4 multiply_reduce_fusion
  620.9 7.1 multiply_convert_fusion
  633.4 9.8 convolution_convert_fusion
  643.2 4.9 copy.171
  653.6 39.1 %reduce-scatter.29.cloned.1.call-done = f32[2,384,768]{2,1,0:T(8,128)} async-done(((f32[2,3072,768]{2,1,0:T(8,128)}), f32[2,384,768]{2,1,0:T(8,128)}) %reduce-scatter.29.cloned.1.call-update) | async-done | bytes 2359312 | tf_op jit(solution)/shard_map/reduce_scatter | solution.py:357
  695.5 4.9 copy.178
  700.5 122.0 %reduce-scatter.25.cloned.1.call-done = f32[2,96,3072]{2,1,0:T(8,128)} async-done(((f32[2,768,3072]{2,1,0:T(8,128)}), f32[2,96,3072]{2,1,0:T(8,128)}) %reduce-scatter.25.cloned.1.call-update) | async-done | bytes 2359312 | tf_op jit(solution)/shard_map/reduce_scatter | solution.py:356
  826.9 5.2 fusion.81
  832.9 5.1 convolution_bitcast_fusion
  838.1 47.0 %reduce-scatter.19.cloned.1.call-done = bf16[4,128,768]{2,1,0:T(8,128)(2,1)} async-done(((bf16[4,512,768]{2,1,0:T(8,128)(2,1)}), bf16[4,128,768]{2,1,0:T(8,128)(2,1)}) %reduce-scatter.19.cloned.1.call-update) | async-done | bytes 786448 | tf_op jit(solution)/shard_map/reduce_scatter | solution.py:222
  886.5 61.0 %reduce-scatter.21.cloned.1.call-done = bf16[4,128,768]{2,1,0:T(8,128)(2,1)} async-done(((bf16[4,512,768]{2,1,0:T(8,128)(2,1)}), bf16[4,128,768]{2,1,0:T(8,128)(2,1)}) %reduce-scatter.21.cloned.1.call-update) | async-done | bytes 786448 | tf_op jit(solution)/shard_map/reduce_scatter | solution.py:225
  949.0 4.9 convolution_bitcast_fusion.1
  953.9 12.5 pad_maximum_fusion.2
  966.4 21.7 %copy.175 = f32[2,768,2304]{2,0,1:T(2,128)} copy(f32[2,768,2304]{1,2,0:T(8,128)} %pad_maximum_fusion.2) | data formatting | bytes 28311552 | tf_op jit(solution)/shard_map/stack | solution.py:337
  988.1 16.8 %reduce-scatter.23.cloned.1.call-done = f32[2,96,768]{2,1,0:T(8,128)} async-done(((f32[2,768,768]{2,1,0:T(8,128)}), f32[2,96,768]{2,1,0:T(8,128)}) %reduce-scatter.23.cloned.1.call-update) | async-done | bytes 589840 | tf_op jit(solution)/shard_map/reduce_scatter | solution.py:355
  1007.5 278.8 %all-reduce.11 = bf16[2,768,2304]{2,0,1:T(2,128)(2,1)} all-reduce(f32[2,768,2304]{2,0,1:T(2,128)} %copy.175), channel_id=6, replica_groups=mesh['dp'=8,'seq'=4] {'dp'}, use_global_device_ids=true, to_apply=%region_35.36.clone | all-reduce | flops 3538944 | bytes 21233664
  1288.1 47.7 %copy.183 = bf16[2,96,2304]{0,1,2:T(8,128)(2,1)} copy(bf16[2,96,2304]{2,0,1:T(2,128)(2,1)S(1)} %dynamic-slice_convert_fusion) | data formatting | bytes 1769472
  1335.9 83.9 %reshape.270 = bf16[2304,192]{1,0:T(8,128)(2,1)} reshape(bf16[2304,96,2]{2,1,0:T(8,128)(2,1)} %bitcast.210) | data formatting | bytes 1769472
  1433.4 5.9 fusion.59
  1440.4 17.2 %all_gather.34 = bf16[2,96,768]{1,0,2:T(2,128)(2,1)S(1)} all-gather(bf16[2,96,192]{1,0,2:T(2,128)(2,1)S(1)} %bitcast.247), channel_id=1, replica_groups=mesh['dp'=8,'seq'=4] {'seq'}, dimensions={2}, use_global_device_ids=true | all-gather | bytes 368640 | tf_op jit(solution)/shard_map/all_gather | solution.py:377
  1458.7 31.4 %reshape.271 = bf16[576,96,2]{2,1,0:T(8,128)(2,1)} reshape(bf16[576,192]{1,0:T(8,128)(2,1)} %reduce-scatter.31.cloned.1.call-done) | data formatting | bytes 442368
  1490.0 10.7 copy.176
  1500.8 31.6 %all_gather.33 = bf16[2,96,2304]{1,0,2:T(2,128)(2,1)S(1)} all-gather(bf16[2,96,576]{1,0,2:T(2,128)(2,1)S(1)} %copy.176), channel_id=1, replica_groups=mesh['dp'=8,'seq'=4] {'seq'}, dimensions={2}, use_global_device_ids=true | all-gather | bytes 1105920 | tf_op jit(solution)/shard_map/all_gather | solution.py:374
  1534.9 5.1 copy.181
  1542.9 110.8 %all-reduce.10.cloned.1.call-done = (f32[2,768]{1,0:T(2,128)}, f32[2,768]{1,0:T(2,128)}, f32[2,768]{1,0:T(2,128)}, f32[2,768]{1,0:T(2,128)}, f32[2,768]{1,0:T(2,...) async-done(((f32[2,768]{1,0:T(2,128)}, f32[2,768]{1,0:T(2,128)}, f32[2,768]{1,0:T(2,128)}, f32[2,768]{1,0:T(2,128)}, ...) | async-done | bytes 73744 | tf_op jit(solution)/shard_map/psum | solution.py:387
  (441 shorter events, 181.3 us)
Async XLA Ops:
  7.2 72.9 %all-gather.9.cloned.1.call-start = ((), (), s32[]{:S(2)}) async-start(), calls=%async_computation.11 | async-start | bytes 3932160 | tf_op jit(solution)/shard_map/all_gather | solution.py:134
  13.7 130.7 %all-gather.7.cloned.1.call-start = ((), (), s32[]{:S(2)}) async-start(), calls=%async_computation.10 | async-start | bytes 3932160 | tf_op jit(solution)/shard_map/all_gather | solution.py:135
  14.5 231.0 %all-gather.13.cloned.1.call-start = ((), (), s32[]{:S(2)}) async-start(), calls=%async_computation.13 | async-start | bytes 3932160 | tf_op jit(solution)/shard_map/all_gather | solution.py:134
  30.8 145.7 %copy-start.56 = (f32[768]{0:T(1024)}, f32[768]{0:T(1024)S(1)}, u32[]{:S(2)}) copy-start(f32[768]{0:T(1024)S(1)} %get-tuple-element.195) | copy-start | bytes 9220
  30.9 145.7 %copy-start.82 = (f32[768]{0:T(1024)}, f32[768]{0:T(1024)S(1)}, u32[]{:S(2)}) copy-start(f32[768]{0:T(1024)S(1)} %get-tuple-element.117) | copy-start | bytes 9220
  30.9 315.8 %copy-start.58 = (f32[768]{0:T(1024)}, f32[768]{0:T(1024)S(1)}, u32[]{:S(2)}) copy-start(f32[768]{0:T(1024)S(1)} %get-tuple-element.196) | copy-start | bytes 9220
  30.9 315.7 %copy-start.84 = (f32[768]{0:T(1024)}, f32[768]{0:T(1024)S(1)}, u32[]{:S(2)}) copy-start(f32[768]{0:T(1024)S(1)} %get-tuple-element.116) | copy-start | bytes 9220
  30.9 293.1 %copy-start.54 = (f32[768]{0:T(1024)}, f32[768]{0:T(1024)S(1)}, u32[]{:S(2)}) copy-start(f32[768]{0:T(1024)S(1)} %get-tuple-element.197) | copy-start | bytes 9220
  30.9 293.1 %copy-start.80 = (f32[768]{0:T(1024)}, f32[768]{0:T(1024)S(1)}, u32[]{:S(2)}) copy-start(f32[768]{0:T(1024)S(1)} %get-tuple-element.111) | copy-start | bytes 9220
  31.2 126.1 %copy-start.64 = (f32[1,3072]{1,0:T(1,128)}, f32[1,3072]{1,0:T(1,128)S(1)}, u32[]{:S(2)}) copy-start(f32[1,3072]{1,0:T(1,128)S(1)} %get-tuple-element.154) | copy-start | bytes 36868
  31.2 294.3 %copy-start.66 = (f32[1,3072]{1,0:T(1,128)}, f32[1,3072]{1,0:T(1,128)S(1)}, u32[]{:S(2)}) copy-start(f32[1,3072]{1,0:T(1,128)S(1)} %get-tuple-element.153) | copy-start | bytes 36868
  179.7 144.4 %copy-start.68 = (f32[512]{0:T(512)}, f32[512]{0:T(512)S(1)}, u32[]{:S(2)}) copy-start(f32[512]{0:T(512)S(1)} %add_rsqrt_fusion.2) | copy-start | bytes 6148
  183.2 126.5 %all-gather.11.cloned.1.call-start = ((), (), s32[]{:S(2)}) async-start(), calls=%async_computation.12 | async-start | bytes 3932160 | tf_op jit(solution)/shard_map/all_gather | solution.py:135
  183.8 300.3 %reduce-scatter.15.cloned.1.call-start = ((), (), s32[]{:S(2)}) async-start(), calls=%async_computation.14 | async-start | bytes 3932160 | tf_op jit(solution)/shard_map/reduce_scatter | solution.py:222
  183.9 166.0 %copy-start.53 = (s32[512]{0:T(512)}, s32[512]{0:T(512)S(1)}, u32[]{:S(2)}) copy-start(s32[512]{0:T(512)S(1)} %add_bitcast_fusion) | copy-start | bytes 6148
  425.2 121.4 %reduce-scatter.17.cloned.1.call-start = ((), (), s32[]{:S(2)}) async-start(), calls=%async_computation.15 | async-start | bytes 3932160 | tf_op jit(solution)/shard_map/reduce_scatter | solution.py:225
  439.7 253.0 %reduce-scatter.29.cloned.1.call-start = ((), (), s32[]{:S(2)}) async-start(), calls=%async_computation.22 | async-start | bytes 21233664 | tf_op jit(solution)/shard_map/reduce_scatter | solution.py:357
  446.7 102.2 %copy-start.16 = (f32[512,768]{1,0:T(8,128)S(1)}, f32[512,768]{1,0:T(8,128)}, u32[]{:S(2)}) copy-start(f32[512,768]{1,0:T(8,128)} %copy-done.14) | copy-start | bytes 4718596
  446.7 102.2 %copy-start.28 = (f32[512,768]{1,0:T(8,128)S(1)}, f32[512,768]{1,0:T(8,128)}, u32[]{:S(2)}) copy-start(f32[512,768]{1,0:T(8,128)} %copy-done.27) | copy-start | bytes 4718596
  446.7 102.2 %copy-start.55 = (f32[768]{0:T(1024)S(1)}, f32[768]{0:T(1024)}, u32[]{:S(2)}) copy-start(f32[768]{0:T(1024)} %copy-done.54) | copy-start | bytes 9220
  446.7 102.2 %copy-start.69 = (f32[512]{0:T(512)S(1)}, f32[512]{0:T(512)}, u32[]{:S(2)}) copy-start(f32[512]{0:T(512)} %copy-done.68) | copy-start | bytes 6148
  566.4 256.0 %reduce-scatter.25.cloned.1.call-start = ((), (), s32[]{:S(2)}) async-start(), calls=%async_computation.19 | async-start | bytes 21233664 | tf_op jit(solution)/shard_map/reduce_scatter | solution.py:356
  596.7 288.3 %reduce-scatter.19.cloned.1.call-start = ((), (), s32[]{:S(2)}) async-start(), calls=%async_computation.16 | async-start | bytes 3932160 | tf_op jit(solution)/shard_map/reduce_scatter | solution.py:222
  633.4 314.1 %reduce-scatter.21.cloned.1.call-start = ((), (), s32[]{:S(2)}) async-start(), calls=%async_computation.17 | async-start | bytes 3932160 | tf_op jit(solution)/shard_map/reduce_scatter | solution.py:225
  648.1 356.8 %reduce-scatter.23.cloned.1.call-start = ((), (), s32[]{:S(2)}) async-start(), calls=%async_computation.18 | async-start | bytes 5308416 | tf_op jit(solution)/shard_map/reduce_scatter | solution.py:355
  653.6 767.8 %all-reduce.8.cloned.1.call-start = ((), (), s32[]{:S(2)}) async-start(), calls=%async_computation.26 | async-start | bytes 2359296
  695.5 130.1 %copy-start.101 = (u32[32]{0:T(128)S(1)}, u32[32]{0:T(128)}, u32[]{:S(2)}) copy-start(u32[32]{0:T(128)} %constant.114) | copy-start | bytes 388
  695.5 131.3 %copy-start.5 = (bf16[4,512,768]{1,2,0:T(8,128)(2,1)S(1)}, bf16[4,512,768]{1,2,0:T(8,128)(2,1)}, u32[]{:S(2)}) copy-start(bf16[4,512,768]{1,2,0:T(8,128)(2,1)} %copy-done.4) | copy-start | bytes 9437188
  700.4 727.8 %reduce-scatter.27.cloned.1.call-start = ((), (), s32[]{:S(2)}) async-start(), calls=%async_computation.20 | async-start | bytes 1474560 | tf_op jit(solution)/shard_map/reduce_scatter | solution.py:366
  825.3 614.0 %reduce-scatter.33.cloned.1.call-start = ((), (), s32[]{:S(2)}) async-start(), calls=%async_computation.25 | async-start | bytes 491520
  832.9 116.0 %copy-start.42 = (bf16[96,8,4,128]{3,1,2,0:T(8,128)(2,1)}, bf16[96,8,4,128]{3,1,2,0:T(8,128)(2,1)S(1)}, u32[]{:S(2)}) copy-start(bf16[96,8,4,128]{3,1,2,0:T(8,128)(2,1)S(1)} %copy.238) | copy-start | bytes 2359300
  832.9 116.0 %copy-start.99 = (bf16[4,128,768]{2,1,0:T(8,128)(2,1)S(1)}, bf16[4,128,768]{2,1,0:T(8,128)(2,1)}, u32[]{:S(2)}) copy-start(bf16[4,128,768]{2,1,0:T(8,128)(2,1)} %param.16) | copy-start | bytes 2359300
  886.5 67.4 %copy-start.43 = (bf16[512,768]{0,1:T(8,128)(2,1)}, bf16[512,768]{0,1:T(8,128)(2,1)S(1)}, u32[]{:S(2)}) copy-start(bf16[512,768]{0,1:T(8,128)(2,1)S(1)} %copy.172) | copy-start | bytes 2359300
  1007.4 451.2 %reduce-scatter.31.cloned.1.call-start = ((), (), s32[]{:S(2)}) async-start(), calls=%async_computation.24 | async-start | bytes 1474560
  1335.8 84.3 %copy-start.100 = (u32[32]{0:T(128)S(1)}, u32[32]{0:T(128)}, u32[]{:S(2)}) copy-start(u32[32]{0:T(128)} %constant.118) | copy-start | bytes 388
  1335.8 87.5 %copy-start.61 = (f32[768]{0:T(1024)S(1)}, f32[768]{0:T(1024)}, u32[]{:S(2)}) copy-start(f32[768]{0:T(1024)} %get-tuple-element.141) | copy-start | bytes 9220
  1335.8 87.5 %copy-start.91 = (f32[768]{0:T(1024)S(1)}, f32[768]{0:T(1024)}, u32[]{:S(2)}) copy-start(f32[768]{0:T(1024)} %get-tuple-element.96) | copy-start | bytes 9220
  1335.8 87.6 %copy-start.90 = (f32[768]{0:T(1024)S(1)}, f32[768]{0:T(1024)}, u32[]{:S(2)}) copy-start(f32[768]{0:T(1024)} %get-tuple-element.105) | copy-start | bytes 9220
  1335.9 87.6 %copy-start.60 = (f32[768]{0:T(1024)S(1)}, f32[768]{0:T(1024)}, u32[]{:S(2)}) copy-start(f32[768]{0:T(1024)} %get-tuple-element.137) | copy-start | bytes 9220
  1335.9 87.6 %copy-start.89 = (f32[768]{0:T(1024)S(1)}, f32[768]{0:T(1024)}, u32[]{:S(2)}) copy-start(f32[768]{0:T(1024)} %get-tuple-element.92) | copy-start | bytes 9220
  1335.9 87.6 %copy-start.88 = (f32[768]{0:T(1024)S(1)}, f32[768]{0:T(1024)}, u32[]{:S(2)}) copy-start(f32[768]{0:T(1024)} %get-tuple-element.103) | copy-start | bytes 9220
  1335.9 88.3 %copy-start.62 = (f32[768]{0:T(1024)S(1)}, f32[768]{0:T(1024)}, u32[]{:S(2)}) copy-start(f32[768]{0:T(1024)} %get-tuple-element.135) | copy-start | bytes 9220
  1335.9 88.3 %copy-start.93 = (f32[768]{0:T(1024)S(1)}, f32[768]{0:T(1024)}, u32[]{:S(2)}) copy-start(f32[768]{0:T(1024)} %get-tuple-element.90) | copy-start | bytes 9220
  1335.9 90.7 %copy-start.38 = (bf16[96,8,4,128]{3,1,2,0:T(8,128)(2,1)S(1)}, bf16[96,8,4,128]{3,1,2,0:T(8,128)(2,1)}, u32[]{:S(2)}) copy-start(bf16[96,8,4,128]{3,1,2,0:T(8,128)(2,1)} %copy.239) | copy-start | bytes 2359300
  1335.9 90.7 %copy-start.40 = (bf16[512,768]{0,1:T(8,128)(2,1)S(1)}, bf16[512,768]{0,1:T(8,128)(2,1)}, u32[]{:S(2)}) copy-start(bf16[512,768]{0,1:T(8,128)(2,1)} %copy.163) | copy-start | bytes 2359300
  1419.8 115.1 %all-gather.17.cloned.1.call-start = ((), (), s32[]{:S(2)}) async-start(), calls=%async_computation.23 | async-start | bytes 1474560 | tf_op jit(solution)/shard_map/all_gather | solution.py:383
  1423.3 116.7 %all-gather.15.cloned.1.call-start = ((), (), s32[]{:S(2)}) async-start(), calls=%async_computation.21 | async-start | bytes 1474560 | tf_op jit(solution)/shard_map/all_gather | solution.py:380
  1428.2 225.5 %all-reduce.10.cloned.1.call-start = ((), (), s32[]{:S(2)}) async-start(), calls=%async_computation.27 | async-start | bytes 147456 | tf_op jit(solution)/shard_map/psum | solution.py:387
  (92 other events, 936.3 us)
Sparse Core Ops, SparseCore 0:
  13.9 66.1 all-gather.8
  82.2 62.1 all-gather.6
  183.3 62.1 all-gather.12
  247.5 62.1 all-gather.10
  425.3 58.7 reduce-scatter.14
  486.3 60.2 reduce-scatter.16
  566.5 126.1 reduce-scatter.28
  696.3 126.1 reduce-scatter.24
  824.8 60.2 reduce-scatter.18
  887.2 60.2 reduce-scatter.20
  951.0 53.9 reduce-scatter.22
  1007.3 55.8 all-reduce.7
  1066.2 28.7 reduce-scatter.26
  1097.8 19.2 reduce-scatter.32
  1419.9 30.5 reduce-scatter.30
  1452.0 30.1 all-gather.16
  1483.6 39.7 all-gather.14
  1530.9 122.8 all-reduce.9
where the time goes:
time: 1690 us; the launch traced here: 1670 us
  waiting for transfers between devices  703 us (42%)
  blocking collectives  360 us (21%)
  local copies, waits for them, and re-layouts  298 us (18%)
  matrix products  212 us (13%)
  other arithmetic  79.4 us (5%)
  between operations  19.9 us (1%)
    unnamed x1, blocking collectives  279 us
    unnamed x267, local copies, waits for them, and re-layouts  201 us
    reduce_scatter x1, waiting for transfers between devices, on_device(): lax.psum_scatter(matrices[2], 'dp', scatter_dimension=1, tiled=True)  122 us
    reduce_scatter x2, waiting for transfers between devices, layer_backward(): lax.psum_scatter(grad_values_all.astype(jnp.bfloat16), 'seq', scatter_dim...  121 us
    psum x1, waiting for transfers between devices, on_device(): lax.psum((vectors[0], vectors[1], vectors[2], vectors[3], vectors[4], vec...  111 us
    all_gather x2, waiting for transfers between devices, layer_forward(): lax.all_gather(keys_local, 'seq', axis=1, tiled=True)  108 us
    all_gather x2, waiting for transfers between devices, layer_forward(): lax.all_gather(values_local, 'seq', axis=1, tiled=True)  104 us
    reduce_scatter x2, waiting for transfers between devices, layer_backward(): lax.psum_scatter(grad_keys_all.astype(jnp.bfloat16), 'seq', scatter_dimen...  79 us
  transfers between devices with their start and end apart: 18, of which 12 were waited for; matrix products, arithmetic and copies ran while one was open for 24% of the time, Pallas kernels for 0%

commit v1 on v0

v1 whole, which is shorter than its diff:
```python
import functools

import jax
import jax.numpy as jnp
from jax import lax
from jax.experimental import pallas as pl
from jax.experimental.pallas import tpu as pltpu
from jax.sharding import PartitionSpec as P

highest = lax.Precision.HIGHEST
loss_scale = 1024.0
HD = 64
norm_eps = 1e-06
FT = 512


def dot(left, right):
    return lax.dot_general(left, right, (((1,), (0,)), ((), ())), preferred_element_type=jnp.float32)


def dot_t(left, right):
    return lax.dot_general(left, right, (((1,), (1,)), ((), ())), preferred_element_type=jnp.float32)


def gelu_pair(x):
    t = 1.0 / (1.0 + 0.23164190 * jnp.abs(x))
    gauss = jnp.exp(-0.5 * x * x)
    poly = t * (0.127414796 + t * (-0.142248368 + t * (0.7107068705 + t * (-0.7265760135 + t * 0.5307027145))))
    tail = poly * gauss
    phi = jnp.where(x >= 0.0, 1.0 - tail, tail)
    return x * phi, phi + x * (gauss * 0.3989422804014327)


def fwd_kernel(
    layers, tok, segc, segr, b_query, b_value, b_out, gain_one, shift_one, b_up, b_down, gain_two, shift_two,
    w_qkv, w_out, w_up, w_down,
    hid_out, o_qkv, o_p, o_rl, o_pv, o_hidT, o_mixT, o_nrmT, o_actT, o_gp, o_n1, o_r1, o_n2, o_r2,
    wq, wo, wu, wd, bias, hid, low, qkv, pb, rl, pv, mix, nrm, gp, n1, r1, n2, r2, hidT, mixT, nrmT, actT, acc,
    wsem, psem, osem,
):
    T, D = tok.shape
    FF = w_up.shape[2]
    for l in range(layers):
        for i, (src, dst) in enumerate(((w_qkv, wq), (w_out, wo), (w_up, wu), (w_down, wd))):
            pltpu.make_async_copy(src.at[l], dst.at[l], wsem.at[l, i]).start()

    def wwait(l, i):
        src, dst = ((w_qkv, wq), (w_out, wo), (w_up, wu), (w_down, wd))[i]
        pltpu.make_async_copy(src.at[l], dst.at[l], wsem.at[l, i]).wait()

    bias[...] = jnp.where(segc[...] == segr[...], 0.0, -1e30)
    hid[...] = tok[...].astype(jnp.float32)
    lane = lax.broadcasted_iota(jnp.int32, (T, 128), 1)
    first = lane < HD

    def transpose(src, dst, n):
        def body(i, c):
            o = pl.multiple_of(i * 128, 128)
            dst[pl.ds(o, 128), :] = src[:, pl.ds(o, 128)].T
            return c
        lax.fori_loop(0, n // 128, body, 0)

    RB = 64

    def rows(fn):
        def body(i, c):
            fn(pl.ds(pl.multiple_of(i * RB, RB), RB))
            return c
        lax.fori_loop(0, T // RB, body, 0)

    outs = []

    def norm(x, gain, shift):
        centre = x - jnp.mean(x, axis=-1, keepdims=True)
        scaled = lax.rsqrt(jnp.mean(centre * centre, axis=-1, keepdims=True) + norm_eps)
        normal = centre * scaled
        return normal * gain + shift, normal, scaled

    def ship(l, src, dst, k):
        c = pltpu.make_async_copy(src, dst.at[l], osem.at[k])
        c.start()
        outs.append(c)

    for l in range(layers):
        low[...] = hid[...].astype(jnp.bfloat16)
        for c in outs:
            c.wait()
        outs.clear()
        wwait(l, 0)
        lb = low[...]
        for k in range(3):
            cols = slice(k * D, (k + 1) * D)
            y = dot(lb, wq[l, :, cols])
            if k == 0:
                y = (y + b_query[l : l + 1, :]) * 0.125
            if k == 2:
                y = y + b_value[l : l + 1, :]
            qkv[:, cols] = y.astype(jnp.bfloat16)
        ship(l, qkv, o_qkv, 0)
        transpose(low, hidT, D)
        ship(l, hidT, o_hidT, 1)

        def pcopy(i, s):
            return pltpu.make_async_copy(pb.at[s], o_p.at[l, pl.ds(2 * i, 2)], psem.at[s])

        def attend(i, c):
            s = lax.rem(i, 2)
            o = pl.multiple_of(i * 128, 128)
            q2, k2, v2 = (qkv[:, pl.ds(o + k * D, 128)] for k in range(3))

            @pl.when(i >= 2)
            def _():
                pcopy(i - 2, s).wait()

            zero = jnp.zeros_like(q2)
            total = None
            recips = []
            for h in range(2):
                sel = first if h == 0 else ~first
                sc = dot_t(jnp.where(sel, q2, zero), k2) + bias[...]
                e = jnp.exp(sc - jnp.max(sc, axis=-1, keepdims=True))
                recips.append(1.0 / jnp.sum(e, axis=-1, keepdims=True))
                p = e.astype(jnp.bfloat16)
                pb[s, h] = p
                part = dot(p, jnp.where(sel, v2, zero))
                total = part if h == 0 else total + part
            r = jnp.where(first, recips[0], recips[1])
            rl[:, pl.ds(o, 128)] = r
            total = total * r
            pv[:, pl.ds(o, 128)] = total
            mix[:, pl.ds(o, 128)] = total.astype(jnp.bfloat16)
            pcopy(i, s).start()
            return c

        n_pairs = D // 128
        lax.fori_loop(0, n_pairs, attend, 0)
        ship(l, rl, o_rl, 2)
        ship(l, pv, o_pv, 3)
        wwait(l, 1)
        acc[...] = dot(mix[...], wo[l])
        transpose(mix, mixT, D)
        ship(l, mixT, o_mixT, 4)

        def first_norm(rs):
            x = hid[rs, :] + acc[rs, :] + b_out[l : l + 1, :]
            y, n, r = norm(x, gain_one[l : l + 1, :], shift_one[l : l + 1, :])
            nrm[rs, :] = y
            low[rs, :] = y.astype(jnp.bfloat16)
            n1[rs, :] = n.astype(jnp.bfloat16)
            r1[rs, :] = jnp.broadcast_to(r, (RB, 128))

        rows(first_norm)
        ship(l, n1, o_n1, 5)
        ship(l, r1, o_r1, 6)
        transpose(low, nrmT, D)
        ship(l, nrmT, o_nrmT, 7)
        wwait(l, 2)
        wwait(l, 3)
        acc[...] = nrm[...]

        def ffn(j, c):
            o = pl.multiple_of(j * FT, FT)
            pre = dot(low[...], wu[l, :, pl.ds(o, FT)]) + b_up[l : l + 1, pl.ds(o, FT)]
            a, g = gelu_pair(pre)
            al = a.astype(jnp.bfloat16)
            gp[:, pl.ds(o, FT)] = g.astype(jnp.bfloat16)
            acc[...] += dot(al, wd[l, pl.ds(o, FT), :])
            actT[pl.ds(o, FT), :] = al.T
            return c

        lax.fori_loop(0, FF // FT, ffn, 0)
        ship(l, gp, o_gp, 8)
        ship(l, actT, o_actT, 9)

        def second_norm(rs):
            x = acc[rs, :] + b_down[l : l + 1, :]
            y, n, r = norm(x, gain_two[l : l + 1, :], shift_two[l : l + 1, :])
            hid[rs, :] = y
            n2[rs, :] = n.astype(jnp.bfloat16)
            r2[rs, :] = jnp.broadcast_to(r, (RB, 128))

        rows(second_norm)
        ship(l, n2, o_n2, 10)
        ship(l, r2, o_r2, 11)
        for i in (n_pairs - 2, n_pairs - 1):
            pcopy(i, i % 2).wait()
    hid_out[...] = hid[...]
    for c in outs:
        c.wait()


def forward(tok, seg, w):
    T, D = tok.shape
    L = w["w_qkv"].shape[0]
    FF = w["w_up"].shape[2]
    bf, f32 = jnp.bfloat16, jnp.float32
    S = jax.ShapeDtypeStruct
    vm = pl.BlockSpec(memory_space=pltpu.VMEM)
    anyspec = pl.BlockSpec(memory_space=pl.ANY)
    H = D // HD
    out_shape = (
        S((T, D), f32), S((L, T, 3 * D), bf), S((L, H, T, T), bf), S((L, T, D), f32), S((L, T, D), f32),
        S((L, D, T), bf), S((L, D, T), bf), S((L, D, T), bf), S((L, FF, T), bf), S((L, T, FF), bf),
        S((L, T, D), bf), S((L, T, 128), f32), S((L, T, D), bf), S((L, T, 128), f32),
    )
    V = pltpu.VMEM
    scratch = [
        V((L, D, 3 * D), bf), V((L, D, D), bf), V((L, D, FF), bf), V((L, FF, D), bf),
        V((T, T), f32), V((T, D), f32), V((T, D), bf), V((T, 3 * D), bf), V((2, 2, T, T), bf),
        V((T, D), f32), V((T, D), f32), V((T, D), bf), V((T, D), f32), V((T, FF), bf),
        V((T, D), bf), V((T, 128), f32), V((T, D), bf), V((T, 128), f32),
        V((D, T), bf), V((D, T), bf), V((D, T), bf), V((FF, T), bf), V((T, D), f32),
        pltpu.SemaphoreType.DMA((L, 4)), pltpu.SemaphoreType.DMA((2,)), pltpu.SemaphoreType.DMA((12,)),
    ]
    return pl.pallas_call(
        functools.partial(fwd_kernel, L),
        out_shape=out_shape,
        in_specs=[vm] * 12 + [anyspec] * 4,
        out_specs=(vm,) + (anyspec,) * 13,
        scratch_shapes=scratch,
        compiler_params=pltpu.CompilerParams(vmem_limit_bytes=60 * 1024 * 1024),
        name="forward",
    )(
        tok, seg.reshape(T, 1), seg.reshape(1, T),
        *(w[k] for k in ("b_query", "b_value", "b_out", "gain_one", "shift_one", "b_up", "b_down", "gain_two", "shift_two")),
        *(w[k] for k in ("w_qkv", "w_out", "w_up", "w_down")),
    )


MESH = pl.DeviceIdType.MESH
C = 256
CORE_SLOTS = 4
SLOTS = 6
LAGS = (0, 1, 3, 5, 7, 9, 11)
VEC_ROWS = 16
WAYS = 8


def low_sum(one, other):
    return (one.astype(jnp.float32) + other.astype(jnp.float32)).astype(jnp.bfloat16)


def remote(src, dst, send_sem, recv_sem, where):
    return pltpu.make_async_remote_copy(
        src_ref=src, dst_ref=dst, send_sem=send_sem, recv_sem=recv_sem, device_id=where, device_id_type=MESH
    )


def bwd_kernel(
    layers, g_in, gain_one, gain_two,
    w_qkv, w_out, w_up, w_down,
    h_qkv, h_p, h_rl, h_pv, h_hidT, h_mixT, h_nrmT, h_actT, h_gp, h_n1, h_r1, h_n2, h_r2,
    out, gt_out, vec_out,
    wq, wo, wu, wd, qkv, pb, rl, pv, hidT, mixT, nrmT, actT, gp, n1, r1, n2, r2,
    acc, second, branch, gm, rhsA, rhsB, vec, vrecv, gb,
    sendc, keepc, recvc, s1, k1, t1, s2, k2, t2, za, zr, zb, zt, zf,
    ldsem, psem, csem, xsem, ysem, zsem, osem, vsem, gsem,
):
    T, D = g_in.shape
    FF = w_up.shape[2]
    R = D // WAYS
    n_ffn = FF // C
    n_att = D // 128
    per = n_ffn + n_att
    n_steps = layers * per
    n_ct = D // C
    n_rb = FF // WAYS // R

    me = lax.axis_index("dp")
    zi = lax.axis_index("seq")
    oc = lax.rem(me, 2)
    ox = lax.rem(lax.div(me, 2), 2)
    oy = lax.rem(lax.div(me, 4), 2)
    core = (me + 1 - 2 * oc, zi)
    xdev = (me + 2 - 4 * ox, zi)
    ydev = (me + 4 - 8 * oy, zi)
    inner = (zi == 1) | (zi == 2)
    outer = (zi == 0) | (zi == 3)
    to_inner = (me, 1 + lax.div(zi, 2))
    across = (me, 3 - zi)
    to_outer = (me, 3 * lax.div(zi, 2))

    barrier = pltpu.get_barrier_semaphore()
    peers = [core, xdev, ydev] + [(me, lax.rem(zi + k, 4)) for k in range(1, 4)]
    for peer in peers:
        pl.semaphore_signal(barrier, inc=1, device_id=peer, device_id_type=MESH)
    pl.semaphore_wait(barrier, len(peers))

    def place(ic, i):
        y = lax.rem(oy + i // 2, 2)
        x = lax.rem(ox + i % 2, 2)
        return 4 * y + 2 * x + lax.rem(oc + ic, 2)

    def turned(src, dst, l):
        return [
            (src.at[l, place(ic, i)], dst.at[ic, pl.ds(i * R, R)]) for ic in range(2) for i in range(4)
        ]

    def group_ffn(l):
        parts = [(w_down.at[l], wd), (w_up.at[l], wu), (h_gp.at[l], gp), (h_n2.at[l], n2), (h_r2.at[l], r2)]
        parts += turned(h_nrmT, nrmT, l)
        for ic in range(2):
            for i in range(4):
                for rb in range(n_rb):
                    parts.append((h_actT.at[l, place(ic, i), rb], actT.at[ic, rb, pl.ds(i * R, R)]))
        return [pltpu.make_async_copy(a, b, ldsem.at[0, k]) for k, (a, b) in enumerate(parts)]

    def group_att(l):
        parts = [(w_out.at[l], wo), (w_qkv.at[l], wq), (h_qkv.at[l], qkv), (h_rl.at[l], rl), (h_pv.at[l], pv)]
        parts += [(h_n1.at[l], n1), (h_r1.at[l], r1)]
        parts += turned(h_hidT, hidT, l) + turned(h_mixT, mixT, l)
        return [pltpu.make_async_copy(a, b, ldsem.at[1, k]) for k, (a, b) in enumerate(parts)]

    def pcopy(l, i):
        s = lax.rem(i, 2)
        return pltpu.make_async_copy(h_p.at[l, pl.ds(2 * i, 2)], pb.at[s], psem.at[s])

    for c in group_ffn(layers - 1) + group_att(layers - 1):
        c.start()

    acc[...] = g_in[...]
    vec[...] = jnp.zeros_like(vec)
    lane = lax.broadcasted_iota(jnp.int32, (T, 128), 1)
    first = lane < HD
    RB = 64

    def rows(fn):
        def body(i, sums):
            return tuple(a + b for a, b in zip(sums, fn(pl.ds(pl.multiple_of(i * RB, RB), RB))))
        zero = jnp.zeros((1, D), jnp.float32)
        return lax.fori_loop(0, T // RB, body, (zero, zero, zero))

    def norm_back(g, n, r, gain):
        e = g * gain
        return r * (e - jnp.mean(e, axis=-1, keepdims=True) - n * jnp.mean(e * n, axis=-1, keepdims=True))

    def col_sum(v):
        return jnp.sum(v.astype(jnp.float32), axis=0, keepdims=True)

    def prologue(l):
        for c in group_ffn(l):
            c.wait()

        def fn(rs):
            g = acc[rs, :]
            n = n2[rs, :].astype(jnp.float32)
            d = norm_back(g, n, r2[rs, :1], gain_two[l])
            acc[rs, :] = d
            low = d.astype(jnp.bfloat16)
            second[rs, :] = low
            return col_sum(low), col_sum(g * n), col_sum(g)

        a, b, c = rows(fn)
        vec[l, 9:10, :] = a
        vec[l, 10:11, :] = b
        vec[l, 11:12, :] = c

    def ffn(l, j, slot):
        o = pl.multiple_of(j * C, C)
        ga = dot_t(second[...], wd[pl.ds(o, C), :])
        gpre = (ga * gp[:, pl.ds(o, C)].astype(jnp.float32)).astype(jnp.bfloat16)
        ct = lax.rem(j, n_ct)
        rb = lax.div(j, n_ct)
        cols = pl.ds(pl.multiple_of(ct * C, C), C)
        vec[l, pl.ds(5 + rb, 1), cols] = col_sum(gpre)
        sec = second[:, cols]
        for ic, buf in ((1, sendc), (0, keepc)):
            buf[slot, 0] = dot(nrmT[ic], gpre).astype(jnp.bfloat16)
            buf[slot, 1] = dot(actT[ic, rb], sec).astype(jnp.bfloat16)
        acc[...] += dot_t(gpre, wu[:, pl.ds(o, C)])

    def middle(l):
        for c in group_att(l):
            c.wait()

        def fn(rs):
            g = acc[rs, :]
            n = n1[rs, :].astype(jnp.float32)
            d = norm_back(g, n, r1[rs, :1], gain_one[l])
            acc[rs, :] = d
            low = d.astype(jnp.bfloat16)
            branch[rs, :] = low
            return col_sum(low), col_sum(g * n), col_sum(g)

        a, b, c = rows(fn)
        vec[l, 2:3, :] = a
        vec[l, 3:4, :] = b
        vec[l, 4:5, :] = c
        gm[...] = (dot_t(branch[...], wo[...]) * rl[...]).astype(jnp.bfloat16)

    def attend(l, i, slot):
        o = pl.multiple_of(i * 128, 128)
        ps = lax.rem(i, 2)
        pcopy(l, i).wait()
        q2, k2, v2 = (qkv[:, pl.ds(o + k * D, 128)] for k in range(3))
        g2 = gm[:, pl.ds(o, 128)]
        weighed = g2.astype(jnp.float32) * pv[:, pl.ds(o, 128)]
        zero = jnp.zeros_like(q2)
        q2t, g2t = q2.T, g2.T
        dq = None
        dkt, dvt = [], []
        for h in range(2):
            sel = first if h == 0 else ~first
            p = pb[ps, h]
            gprob = dot_t(jnp.where(sel, g2, zero), v2)
            centre = jnp.sum(jnp.where(sel, weighed, 0.0), axis=-1, keepdims=True)
            ds = (p.astype(jnp.float32) * (gprob - centre)).astype(jnp.bfloat16)
            part = dot(ds, jnp.where(sel, k2, zero))
            dq = part if h == 0 else dq + part
            dkt.append(dot(q2t[h * HD : (h + 1) * HD], ds))
            dvt.append(dot(g2t[h * HD : (h + 1) * HD], p))
        dq = (dq * 0.125).astype(jnp.bfloat16)
        dk = jnp.concatenate(dkt, axis=0).astype(jnp.bfloat16).T
        dv = jnp.concatenate(dvt, axis=0).astype(jnp.bfloat16).T
        vec[l, 0:1, pl.ds(o, 128)] = col_sum(dq)
        vec[l, 1:2, pl.ds(o, 128)] = col_sum(dv)
        rhsA[:, :128] = dq
        rhsA[:, 128:] = dk
        rhsB[:, :128] = dv
        rhsB[:, 128:] = branch[:, pl.ds(o, 128)]
        for ic, buf in ((1, sendc), (0, keepc)):
            buf[slot, 0] = dot(hidT[ic], rhsA[...]).astype(jnp.bfloat16)
            buf[slot, 1, :, :128] = dot(hidT[ic], rhsB[:, :128]).astype(jnp.bfloat16)
            buf[slot, 1, :, 128:] = dot(mixT[ic], rhsB[:, 128:]).astype(jnp.bfloat16)
        acc[...] += (
            dot_t(dq, wq[:, pl.ds(o, 128)]) + dot_t(dk, wq[:, pl.ds(o + D, 128)]) + dot_t(dv, wq[:, pl.ds(o + 2 * D, 128)])
        )

        @pl.when(i + 2 < n_att)
        def _():
            pcopy(l, i + 2).start()

    def copy_core(u):
        s = lax.rem(u, CORE_SLOTS)
        return remote(sendc.at[s], recvc.at[s], csem.at[0, s], csem.at[1, s], core)

    def copies_one(u):
        s = lax.rem(u, SLOTS)
        return [
            remote(s1.at[s, k], t1.at[s, k], xsem.at[0, k, s], xsem.at[1, k, s], (xdev, ydev)[k]) for k in range(2)
        ]

    def copies_two(u):
        s = lax.rem(u, SLOTS)
        return [
            remote(s2.at[s, k], t2.at[s, k], ysem.at[0, k, s], ysem.at[1, k, s], (ydev, xdev)[k]) for k in range(2)
        ]

    def copy_in(u):
        s = lax.rem(u, SLOTS)
        return remote(za.at[s], zr.at[s], zsem.at[0, s], zsem.at[1, s], to_inner)

    def copy_across(u):
        s = lax.rem(u, SLOTS)
        return remote(zb.at[s], zt.at[s], zsem.at[2, s], zsem.at[3, s], across)

    def copy_out(u):
        s = lax.rem(u, SLOTS)
        return remote(zf.at[s], out.at[u], zsem.at[4, s], zsem.at[5, s], to_outer)

    def copy_home(u):
        s = lax.rem(u, SLOTS)
        return pltpu.make_async_copy(zf.at[s], out.at[u], osem.at[s])

    def at(t, stage):
        u = t - LAGS[stage]
        return u, (u >= 0) & (u < n_steps)

    def stage_one(u):
        s = lax.rem(u, CORE_SLOTS)
        d = lax.rem(u, SLOTS)
        copy_core(u).wait()
        for k in range(2):
            sent, kept = ((1, 3), (0, 2)) if k == 0 else ((2, 3), (0, 1))
            for n, (a, b) in enumerate(zip(sent, kept)):
                to = pl.ds(n * R, R)
                s1[d, k, to] = low_sum(keepc[s, k, pl.ds(a * R, R)], recvc[s, k, pl.ds(a * R, R)])
                k1[d, k, to] = low_sum(keepc[s, k, pl.ds(b * R, R)], recvc[s, k, pl.ds(b * R, R)])
        for c in copies_one(u):
            c.start()

    def stage_two(u):
        d = lax.rem(u, SLOTS)
        for c in copies_one(u):
            c.wait()
        for k in range(2):
            s2[d, k] = low_sum(k1[d, k, pl.ds(R, R)], t1[d, k, pl.ds(R, R)])
            k2[d, k] = low_sum(k1[d, k, pl.ds(0, R)], t1[d, k, pl.ds(0, R)])
        for c in copies_two(u):
            c.start()

    def stage_three(u):
        d = lax.rem(u, SLOTS)
        for c in copies_two(u):
            c.wait()
        za[d] = low_sum(k2[d], t2[d])

        @pl.when(outer)
        def _():
            copy_in(u).start()

    def stage_four(u):
        d = lax.rem(u, SLOTS)

        @pl.when(outer)
        def _():
            copy_in(u).wait_send()

        @pl.when(inner)
        def _():
            copy_in(u).wait_recv()
            zb[d] = low_sum(za[d], zr[d])
            copy_across(u).start()

    def stage_five(u):
        d = lax.rem(u, SLOTS)

        @pl.when(inner)
        def _():
            copy_across(u).wait()
            zf[d] = low_sum(zb[d], zt[d])
            copy_out(u).start()
            copy_home(u).start()

    def stage_six(u):
        @pl.when(inner)
        def _():
            copy_out(u).wait_send()
            copy_home(u).wait()

        @pl.when(outer)
        def _():
            copy_out(u).wait_recv()

    stages = (None, stage_one, stage_two, stage_three, stage_four, stage_five, stage_six)

    swaps = (core, xdev, ydev)

    def vec_copy(k):
        where = swaps[k] if k < 3 else (to_inner, across, to_outer)[k - 3]
        return remote(vec, vrecv.at[k], vsem.at[0, k], vsem.at[1, k], where)

    def vec_step(k):
        if 1 <= k <= 3:
            vec_copy(k - 1).wait()
            vec[...] += vrecv[k - 1]
        if k < 3:
            vec_copy(k).start()
        if k == 3:
            @pl.when(outer)
            def _():
                vec_copy(3).start()
        if k == 4:
            @pl.when(outer)
            def _():
                vec_copy(3).wait_send()

            @pl.when(inner)
            def _():
                vec_copy(3).wait_recv()
                vec[...] += vrecv[3]
                vec_copy(4).start()
        if k == 5:
            @pl.when(inner)
            def _():
                vec_copy(4).wait()
                vec[...] += vrecv[4]
                vec_copy(5).start()
        if k == 6:
            @pl.when(inner)
            def _():
                vec_copy(5).wait_send()
                vec_out[...] = vec[...]

            @pl.when(outer)
            def _():
                vec_copy(5).wait_recv()
                vec_out[...] = vrecv[5]

    part = T // 4

    def gt_copy(k):
        peer = lax.rem(zi + k, 4)
        src = gb.at[pl.ds(pl.multiple_of(peer * part, part), part)]
        if k == 0:
            return pltpu.make_async_copy(src, gt_out.at[zi], gsem.at[0, 0])
        return remote(src, gt_out.at[zi], gsem.at[0, k], gsem.at[1, k], (me, peer))

    def step(t, carry):
        for k in range(6, 0, -1):
            u, live = at(t, k)

            @pl.when(live)
            def _(k=k, u=u):
                stages[k](u)

        l = layers - 1 - lax.div(t, per)
        s = lax.rem(t, per)
        slot = lax.rem(t, CORE_SLOTS)
        busy = t < n_steps

        @pl.when(busy & (s == 0))
        def _():
            prologue(l)

        @pl.when(busy & (s == 0) & (l < layers - 1))
        def _():
            for c in group_att(l):
                c.start()

        @pl.when(busy & (s < n_ffn))
        def _():
            ffn(l, s, slot)

        @pl.when(busy & (s == n_ffn - 2))
        def _():
            pcopy(l, jnp.int32(0)).start()
            pcopy(l, jnp.int32(1)).start()

        @pl.when(busy & (s == n_ffn) & (l > 0))
        def _():
            for c in group_ffn(l - 1):
                c.start()

        @pl.when(busy & (s == n_ffn))
        def _():
            middle(l)

        @pl.when(busy & (s >= n_ffn))
        def _():
            attend(l, s - n_ffn, slot)

        @pl.when(busy)
        def _():
            copy_core(t).start()

        @pl.when(t == n_steps)
        def _():
            gb[...] = acc[...].astype(jnp.bfloat16)
            for k in range(4):
                gt_copy(k).start()

        for k in range(7):
            @pl.when(t == n_steps + k)
            def _(k=k):
                vec_step(k)

        return carry

    lax.fori_loop(0, n_steps + LAGS[6] + 1, step, 0)
    for k in range(4):
        gt_copy(k).wait()


def backward(grad_hidden, res, w):
    T, D = grad_hidden.shape
    L = w["w_qkv"].shape[0]
    FF = w["w_up"].shape[2]
    qkv, p, rl, pv, hidT, mixT, nrmT, actT, gp, n1, r1, n2, r2 = res
    bf, f32 = jnp.bfloat16, jnp.float32
    S = jax.ShapeDtypeStruct
    V = pltpu.VMEM
    vm = pl.BlockSpec(memory_space=pltpu.VMEM)
    anyspec = pl.BlockSpec(memory_space=pl.ANY)
    R = D // WAYS
    n_rb = FF // WAYS // R
    n_steps = L * (FF // C + D // 128)
    U = 4 * R
    dma = pltpu.SemaphoreType.DMA
    scratch = [
        V((D, 3 * D), bf), V((D, D), bf), V((D, FF), bf), V((FF, D), bf),
        V((T, 3 * D), bf), V((2, 2, T, T), bf), V((T, D), f32), V((T, D), f32),
        V((2, U, T), bf), V((2, U, T), bf), V((2, U, T), bf), V((2, n_rb, U, T), bf),
        V((T, FF), bf), V((T, D), bf), V((T, 128), f32), V((T, D), bf), V((T, 128), f32),
        V((T, D), f32), V((T, D), bf), V((T, D), bf), V((T, D), bf), V((T, C), bf), V((T, C), bf),
        V((L, VEC_ROWS, D), f32), V((6, L, VEC_ROWS, D), f32), V((T, D), bf),
        V((CORE_SLOTS, 2, U, C), bf), V((CORE_SLOTS, 2, U, C), bf), V((CORE_SLOTS, 2, U, C), bf),
        V((SLOTS, 2, 2 * R, C), bf), V((SLOTS, 2, 2 * R, C), bf), V((SLOTS, 2, 2 * R, C), bf),
        V((SLOTS, 2, R, C), bf), V((SLOTS, 2, R, C), bf), V((SLOTS, 2, R, C), bf),
        V((SLOTS, 2, R, C), bf), V((SLOTS, 2, R, C), bf), V((SLOTS, 2, R, C), bf),
        V((SLOTS, 2, R, C), bf), V((SLOTS, 2, R, C), bf),
        dma((2, 16 + 8 * n_rb)), dma((2,)), dma((2, CORE_SLOTS)), dma((2, 2, SLOTS)), dma((2, 2, SLOTS)),
        dma((6, SLOTS)), dma((SLOTS,)), dma((2, 6)), dma((2, 4)),
    ]
    return pl.pallas_call(
        functools.partial(bwd_kernel, L),
        out_shape=(
            S((n_steps, 2, R, C), bf), S((4, T // 4, D), bf), S((L, VEC_ROWS, D), f32),
        ),
        in_specs=[vm] * 3 + [anyspec] * 17,
        out_specs=(anyspec, anyspec, vm),
        scratch_shapes=scratch,
        compiler_params=pltpu.CompilerParams(
            vmem_limit_bytes=62 * 1024 * 1024, collective_id=0, has_side_effects=True
        ),
        name="backward",
    )(
        grad_hidden, w["gain_one"].reshape(L, 1, D), w["gain_two"].reshape(L, 1, D),
        *(w[k] for k in ("w_qkv", "w_out", "w_up", "w_down")),
        qkv, p, rl, pv, hidT, mixT, nrmT, actT, gp, n1, r1, n2, r2,
    )


def pooled_loss(pooled_sums, counts, pair_local):
    embed = pooled_sums / counts[:, None]
    unit = embed * lax.rsqrt(jnp.sum(embed * embed, axis=-1, keepdims=True) + norm_eps)
    logits = 20.0 * jnp.dot(unit, unit.T, precision=highest)
    chosen = pair_local[:, None] == jnp.arange(pair_local.shape[0], dtype=jnp.int32)[None, :]
    picked = jnp.sum(jnp.where(chosen, logits, 0.0), axis=-1)
    return jnp.mean(jax.nn.logsumexp(logits, axis=-1) - picked)


NAMES = (
    "w_qkv",
    "b_query",
    "b_value",
    "w_out",
    "b_out",
    "gain_one",
    "shift_one",
    "w_up",
    "b_up",
    "w_down",
    "b_down",
    "gain_two",
    "shift_two",
)


def by_class(array, block, ways):
    layers, rows, tokens_here = array.shape
    if ways == 1:
        return array.reshape(layers, WAYS, -1, tokens_here)
    array = array.reshape(layers, ways, WAYS, block, tokens_here)
    return jnp.swapaxes(array, 1, 2).reshape(layers, WAYS, -1, tokens_here)


def on_device(dp_count, tokens, segment_ids, pair_ids, *weights):
    w = dict(zip(NAMES, weights))
    layer_count, model_width, _ = w["w_qkv"].shape
    hidden_units = w["w_up"].shape[2]
    seg_count = pair_ids.shape[0]
    local_segs = seg_count // tokens.shape[0]
    ways = dp_count // WAYS
    row_tokens = lax.all_to_all(tokens, "seq", 0, 1, tiled=True)[0]
    row_ids = lax.all_to_all(segment_ids, "seq", 0, 1, tiled=True)[0]
    hidden, *res = forward(row_tokens, row_ids, w)
    for place in (4, 5, 6):
        res[place] = by_class(res[place], model_width // dp_count, ways)
    block = model_width // WAYS
    acts = by_class(res[7], hidden_units // dp_count, ways)
    res[7] = acts.reshape(layer_count, WAYS, -1, block, acts.shape[-1])
    member = (
        row_ids[:, None] == jnp.arange(local_segs, dtype=jnp.int32)[None, :]
    ).astype(jnp.float32)
    pooled_sums = jnp.einsum("ts,td->sd", member, hidden, precision=highest)
    counts = jnp.sum(member, axis=0)
    pooled_sums = lax.all_gather(pooled_sums, "seq", axis=0, tiled=True)
    counts = lax.all_gather(counts, "seq", axis=0, tiled=True)
    loss_value, pullback = jax.vjp(
        lambda sums_in: pooled_loss(sums_in, counts, pair_ids), pooled_sums
    )
    grad_sums = pullback(jnp.float32(loss_scale))[0]
    grad_sums = lax.dynamic_slice_in_dim(
        grad_sums, lax.axis_index("seq") * local_segs, local_segs, 0
    )
    grad_hidden = jnp.einsum("ts,sd->td", member, grad_sums, precision=highest)
    units, grad_tokens, vec = backward(grad_hidden, res, w)
    if ways > 1:
        groups = [[low + WAYS * high for high in range(ways)] for low in range(WAYS)]
        vec = lax.psum(vec, "dp", axis_index_groups=groups)
    matrices = unpack(units, layer_count, model_width, hidden_units)
    if ways > 1:
        matrices = [
            lax.psum_scatter(
                matrix, "dp", scatter_dimension=1, axis_index_groups=groups, tiled=True
            )
            for matrix in matrices
        ]
    g_qkv, g_out, g_up, g_down = (matrix.astype(jnp.float32) for matrix in matrices)
    up_rows = hidden_units // model_width
    vectors = [vec[:, row] for row in (0, 1, 2, 3, 4)]
    b_up = vec[:, 5 : 5 + up_rows].reshape(layer_count, hidden_units)
    b_down, gain_two, shift_two = (vec[:, 5 + up_rows + row] for row in range(3))
    return (
        loss_value.reshape(1),
        grad_tokens.astype(jnp.float32),
        g_qkv,
        vectors[0],
        vectors[1],
        g_out,
        vectors[2],
        vectors[3],
        vectors[4],
        g_up,
        b_up,
        g_down,
        b_down,
        gain_two,
        shift_two,
    )


def unpack(units, layer_count, model_width, hidden_units):
    block = model_width // WAYS
    n_ffn = hidden_units // C
    n_att = model_width // 128
    n_ct = model_width // C
    units = units.reshape(layer_count, n_ffn + n_att, 2, block, C)[::-1]
    up = units[:, :n_ffn, 0].transpose(0, 2, 1, 3).reshape(layer_count, block, hidden_units)
    down = units[:, :n_ffn, 1].reshape(layer_count, -1, n_ct, block, C)
    down = down.transpose(0, 1, 3, 2, 4).reshape(layer_count, -1, model_width)
    att = units[:, n_ffn:].reshape(layer_count, n_att, 2, block, 2, 128)
    att = att.transpose(0, 3, 2, 4, 1, 5).reshape(layer_count, block, 4, model_width)
    qkv = att[:, :, :3].reshape(layer_count, block, 3 * model_width)
    return [qkv, att[:, :, 3], up, down]


def solution(mesh):
    return jax.shard_map(
        functools.partial(on_device, mesh.shape["dp"]),
        mesh=mesh,
        in_specs=(P("dp", "seq", None), P("dp", "seq"), P("dp")) + (P(),) * 13,
        out_specs=(
            P("dp"),
            P("dp", "seq", None),
            P(None, "dp", None),
            P(),
            P(),
            P(None, "dp", None),
            P(),
            P(),
            P(),
            P(None, "dp", None),
            P(),
            P(None, "dp", None),
            P(),
            P(),
            P(),
        ),
        check_vma=False,
    )
```

time: 1690 us -> 336 us (0.20)
  waiting for transfers between devices: 703 us -> 1.28 us
  blocking collectives: 360 us -> 40.7 us
  local copies, waits for them, and re-layouts: 298 us -> 28.7 us
  Pallas kernels: 0 us -> 249 us
  matrix products: 212 us -> 5.06 us
  other arithmetic: 79.4 us -> 3.94 us
    reduce_scatter x8 -> x0, waiting for transfers between devices: 378 us -> none  [the longest x1 122 us: on_device(): lax.psum_scatter(matrices[2], 'dp', scatter_dimension=1, tiled=True)]
    unnamed x1, blocking collectives: 279 us -> 14.1 us
    pallas_call x0 -> x2, Pallas kernels: none -> 249 us  [the longest x1 187 us: backward(): pl.pallas_call(functools.partial(bwd_kernel, L), out_shape=(S((n_steps, 2...]
    all_gather x6 -> x0, waiting for transfers between devices: 213 us -> none  [the longest x2 108 us: layer_forward(): lax.all_gather(keys_local, 'seq', axis=1, tiled=True)]
    dot_general x36 -> x0, matrix products: 205 us -> none  [the longest x8 46.2 us: times_transpose(): lax.dot_general(left, right, (((1,), (1,)), ((), ())), preferred_element_...]
    unnamed x267 -> x41, local copies, waits for them, and re-layouts: 201 us -> 11.9 us
    psum x1 -> x0, waiting for transfers between devices: 111 us -> none  [on_device(): lax.psum((vectors[0], vectors[1], vectors[2], vectors[3], vectors[4], vec...]
    all_gather x3 -> x1, blocking collectives: 62.5 us -> 14.7 us  [on_device(): pooled_sums = lax.all_gather(pooled_sums, 'seq', axis=0, tiled=True)]
  transfers between devices with their start and end apart: 18 -> 1, of which waited for: 12 -> 1; matrix products, arithmetic and copies ran while one was open for 24% -> 1% of each run, Pallas kernels for 0% -> 0%
where the time goes in v1:
time: 336 us
  Pallas kernels  249 us (74%)
  blocking collectives  40.7 us (12%)
  local copies, waits for them, and re-layouts  28.7 us (9%)
  matrix products  5.06 us (2%)
  other arithmetic  3.94 us (1%)
  starting transfers between devices  3.5 us (1%)
  between operations  3.36 us (1%)
    pallas_call x1, Pallas kernels, backward(): pl.pallas_call(functools.partial(bwd_kernel, L), out_shape=(S((n_steps, 2...  187 us
    pallas_call x1, Pallas kernels, forward(): pl.pallas_call(functools.partial(fwd_kernel, L), out_shape=out_shape, in_...  62 us
    all_gather x1, blocking collectives, on_device(): pooled_sums = lax.all_gather(pooled_sums, 'seq', axis=0, tiled=True)  14.7 us
    unnamed x1, blocking collectives  14.1 us
    all_to_all x1, blocking collectives, on_device(): row_ids = lax.all_to_all(segment_ids, 'seq', 0, 1, tiled=True)[0]  11.9 us
    unnamed x41, local copies, waits for them, and re-layouts  11.9 us
    convert_element_type x4, local copies, waits for them, and re-layouts, on_device(): matrix.astype(jnp.float32)  7.48 us
  transfers between devices with their start and end apart: 1, of which 1 were waited for; matrix products, arithmetic and copies ran while one was open for 1% of the time, Pallas kernels for 0%

profile of v1, /device:TPU:0, one launch (start us, length us, event | category | flops | bytes accessed | tf_op | source)
XLA Modules:
  0.0 335.8 jit_solution(15854104711735640359)
XLA Ops:
  0.7 11.9 %all_to_all.25 = s32[4,1,128]{2,1,0:T(1,128)S(1)} all-to-all(s32[4,1,128]{2,1,0:T(1,128)} %bitcast.72), channel_id=1, replica_groups=mesh['dp'=8,'seq'=4] {'seq'}, dimensions={0} | all-to-all | bytes 4096 | tf_op jit(solution)/shard_map/all_to_all | solution.py:746
  12.6 3.5 %all-to-all-start.1 = ((bf16[4,128,768]{2,1,0:T(8,128)(2,1)}), bf16[4,128,768]{2,1,0:T(8,128)(2,1)S(1)}, u32[]{:S(2)}, u32[]{:S(2)}) async-start(bf16[4,128,768]{2,1,0:T(8,128)(2,1)} %param.16), calls=%async_computation.1 | async-start | bytes 1572864 | tf_op jit(solution)/shard_map/all_to_all | solution.py:745
  16.1 0.6 reshape.109.gain_one
  16.7 0.6 reshape.110.gain_two
  17.3 0.6 dynamic-slice
  18.6 0.9 copy.49.segc
  19.4 0.1 convert_reduce_fusion
  19.6 0.2 dynamic-update-slice
  19.8 14.1 %all-reduce = f32[32]{0:T(128)S(1)} all-reduce(f32[32]{0:T(128)S(1)} %dynamic-update-slice), channel_id=1, replica_groups=mesh['dp'=8,'seq'=4] {'seq'}, use_global_device_ids=true, to_apply=%add | all-reduce | flops 32 | bytes 256
  34.0 1.3 all-to-all-done.1
  35.3 0.9 copy-done
  36.2 62.0 %forward.1 = (f32[512,768]{1,0:T(8,128)}, bf16[2,512,2304]{2,1,0:T(8,128)(2,1)}, bf16[2,12,512,512]{3,2,1,0:T(8,128)(2,1)}, f32[2,512,768]{2,1,0:T(8,128)}, f32[...) custom-call(bf16[512,768]{1,0:T(8,128)(2,1)} %bitcast.61, ...), custom_call_target="tpu_custom_call" | custom-call | tf_op jit(solution)/shard_map/forward/pallas_call | solution.py:215
  98.2 2.0 fusion.11
  100.3 14.7 %all_gather.6 = f32[32,768]{1,0:T(8,128)S(1)} all-gather(f32[8,768]{1,0:T(8,128)S(1)} %fusion.11), channel_id=1, replica_groups=mesh['dp'=8,'seq'=4] {'seq'}, dimensions={0}, use_global_device_ids=true | all-gather | bytes 122880 | tf_op jit(solution)/shard_map/all_gather | solution.py:758
  115.0 0.2 multiply_reduce_fusion.1
  115.2 0.1 dynamic-slice.1
  115.3 0.3 fusion.40
  115.6 0.6 fusion.30
  116.2 0.3 fusion.2
  116.5 0.4 multiply_reduce_fusion
  117.0 0.1 dynamic-slice.2
  117.0 2.0 fusion.9.g_in
  119.0 187.2 %backward.1 = (bf16[36,2,96,256]{3,2,1,0:T(8,128)(2,1)}, bf16[4,128,768]{2,1,0:T(8,128)(2,1)}, f32[2,16,768]{2,1,0:T(8,128)}) custom-call(f32[512,768]{1,0:T(8,128)} %fusion.9.g_in, f32[2,1,768]{2,1,0:T(1,128)} %reshape.109.gain_one, f32[2,1,768]{2,1,0:T(1,128)} %reshape.110.gain_two, bf16[2,768,2304]{2,1,0:T(8,128)(2,1)} %w_qkv.3, ...), custom_call_target="tpu_custom_call" | custom-call | tf_op jit(solution)/shard_map/backward/pallas_call | solution.py:685
  306.2 1.5 slice_bitcast_fusion.2
  307.7 1.8 fusion.39
  309.5 1.4 slice.68
  310.8 3.2 slice_bitcast_fusion
  314.0 0.1 slice.52
  314.1 0.3 reshape.115
  314.4 0.8 copy.50
  315.3 1.4 reshape.116
  316.7 0.9 fusion
  317.5 0.1 convert_bitcast_fusion.2
  317.7 0.6 copy.66
  318.3 0.4 copy-done.1
  318.7 1.3 convert_element_type.43
  320.0 1.3 slice.64
  321.3 1.3 copy.65
  322.6 0.3 convert_bitcast_fusion.1
  322.9 1.6 copy.54
  324.5 2.9 reshape.121
  327.4 2.0 copy.63
  329.4 0.4 convert_bitcast_fusion
  329.9 1.7 reshape.120
  332.2 0.6 copy_bitcast_fusion
  332.8 0.6 copy_bitcast_fusion.2
  333.4 0.6 copy_bitcast_fusion.4
  334.0 0.6 copy_bitcast_fusion.6
  (34 shorter events, 0.2 us)
Async XLA Ops:
  0.6 16.7 %copy-start.14 = (u32[32]{0:T(128)S(1)}, u32[32]{0:T(128)}, u32[]{:S(2)}) copy-start(u32[32]{0:T(128)} %constant.35) | copy-start | bytes 388
  0.7 15.5 %copy-start.5 = (f32[2,768]{1,0:T(2,128)S(1)}, f32[2,768]{1,0:T(2,128)}, u32[]{:S(2)}) copy-start(f32[2,768]{1,0:T(2,128)} %gain_one.1) | copy-start | bytes 18436
  0.7 16.1 %copy-start.6 = (f32[2,768]{1,0:T(2,128)S(1)}, f32[2,768]{1,0:T(2,128)}, u32[]{:S(2)}) copy-start(f32[2,768]{1,0:T(2,128)} %gain_two.1) | copy-start | bytes 18436
  12.6 22.7 %copy-start.3 = (s32[4,1,128]{2,1,0:T(1,128)}, s32[4,1,128]{2,1,0:T(1,128)S(1)}, u32[]{:S(2)}) copy-start(s32[4,1,128]{2,1,0:T(1,128)S(1)} %all_to_all.25) | copy-start | bytes 6148
  12.6 22.6 %all-to-all-start.1 = ((bf16[4,128,768]{2,1,0:T(8,128)(2,1)}), bf16[4,128,768]{2,1,0:T(8,128)(2,1)S(1)}, u32[]{:S(2)}, u32[]{:S(2)}) async-start(bf16[4,128,768]{2,1,0:T(8,128)(2,1)} %param.16), calls=%async_computation.1 | async-start | bytes 1572864 | tf_op jit(solution)/shard_map/all_to_all | solution.py:745
  35.3 0.9 copy-start
  98.2 17.4 %copy-start.13 = (s32[32]{0:T(128)S(1)}, s32[32]{0:T(128)}, u32[]{:S(2)}) copy-start(s32[32]{0:T(128)} %param.18) | copy-start | bytes 388
  98.2 18.8 %copy-start.4 = (s32[4,1,128]{2,1,0:T(1,128)S(1)}, s32[4,1,128]{2,1,0:T(1,128)}, u32[]{:S(2)}) copy-start(s32[4,1,128]{2,1,0:T(1,128)} %copy-done.3) | copy-start | bytes 6148
  316.7 1.0 copy-start.2
  317.5 1.1 copy-start.1
  329.8 2.4 copy-start.11
  329.8 2.4 copy-start.12
  329.8 3.0 copy-start.9
  329.8 3.0 copy-start.10
  329.9 3.6 %copy-start.7 = (f32[2,1,768]{2,1,0:T(1,128)S(1)}, f32[2,1,768]{2,1,0:T(1,128)}, u32[]{:S(2)}) copy-start(f32[2,1,768]{2,1,0:T(1,128)} %get-tuple-element.59) | copy-start | bytes 18436
  329.9 3.6 %copy-start.8 = (f32[2,1,768]{2,1,0:T(1,128)S(1)}, f32[2,1,768]{2,1,0:T(1,128)}, u32[]{:S(2)}) copy-start(f32[2,1,768]{2,1,0:T(1,128)} %get-tuple-element.60) | copy-start | bytes 18436

commit v2 on v1

v2 whole, which is shorter than its diff:
```python
import functools

import jax
import jax.numpy as jnp
from jax import lax
from jax.experimental import pallas as pl
from jax.experimental.pallas import tpu as pltpu
from jax.sharding import PartitionSpec as P

HIGHEST = lax.Precision.HIGHEST
MESH = pl.DeviceIdType.MESH
LOSS_SCALE = 1024.0
NORM_EPS = 1e-06
HD = 64
WIDE = 512
C = 256
WAYS = 8
QUEUE = 18
SLOTS = 6
LAGS = (0, 1, 3, 5, 7, 9, 11)
PACE = (2, 3)
VEC_ROWS = 16
ROW_BLOCK = 64


def dot(left, right, precision=None):
    return lax.dot_general(
        left,
        right,
        (((1,), (0,)), ((), ())),
        precision=precision,
        preferred_element_type=jnp.float32,
    )


def dot_t(left, right, precision=None):
    return lax.dot_general(
        left,
        right,
        (((1,), (1,)), ((), ())),
        precision=precision,
        preferred_element_type=jnp.float32,
    )


def remote(src, dst, send_sem, recv_sem, where):
    return pltpu.make_async_remote_copy(
        src_ref=src,
        dst_ref=dst,
        send_sem=send_sem,
        recv_sem=recv_sem,
        device_id=where,
        device_id_type=MESH,
    )


def greet(peers):
    barrier = pltpu.get_barrier_semaphore()
    for peer in peers:
        pl.semaphore_signal(barrier, inc=1, device_id=peer, device_id_type=MESH)
    pl.semaphore_wait(barrier, len(peers))


def gelu_pair(x):
    t = 1.0 / (1.0 + 0.23164190 * jnp.abs(x))
    gauss = jnp.exp(-0.5 * x * x)
    poly = t * (
        0.127414796
        + t * (-0.142248368 + t * (0.7107068705 + t * (-0.7265760135 + t * 0.5307027145)))
    )
    tail = poly * gauss
    phi = jnp.where(x >= 0.0, 1.0 - tail, tail)
    return x * phi, phi + x * (gauss * 0.3989422804014327)


def norm(x, gain, shift):
    centre = x - jnp.mean(x, axis=-1, keepdims=True)
    scaled = lax.rsqrt(jnp.mean(centre * centre, axis=-1, keepdims=True) + NORM_EPS)
    normal = centre * scaled
    return normal * gain + shift, normal, scaled


def fwd_kernel(
    layers, segs,
    tok, ids, pair, b_query, b_value, b_out, gain_one, shift_one, b_up, b_down, gain_two, shift_two,
    w_qkv, w_out, w_up, w_down,
    grad_out, loss_out, o_qkv, o_p, o_pv, o_hidT, o_mixT, o_nrmT, o_actT, o_gp, o_n1, o_r1, o_n2, o_r2,
    wq, wo, wu, wd, bias, hid, low, idbuf, qkv, pb, pv, mix, nrm, gp, n1, r1, n2, r2,
    hidT, mixT, nrmT, actT, acc, ubuf, gbuf,
    wsem, psem, osem, tsem, usem,
):
    T, D = hid.shape
    FF = w_up.shape[2]
    piece = tok.shape[1]
    parts = T // piece
    me = lax.axis_index("dp")
    zi = lax.axis_index("seq")
    pairs = ((w_qkv, wq), (w_out, wo), (w_up, wu), (w_down, wd))

    def wcopy(l, i):
        return pltpu.make_async_copy(pairs[i][0].at[l], pairs[i][1].at[l], wsem.at[l, i])

    def peer(k):
        return lax.rem(zi + k, parts)

    mine = pl.ds(pl.multiple_of(zi * piece, piece), piece)

    def tcopy(k, n):
        src, dst = ((tok, low.at[mine]), (ids, idbuf.at[zi]))[n]
        if k == 0:
            return pltpu.make_async_copy(src.at[zi], dst, tsem.at[n, 0, 0])
        return remote(src.at[peer(k)], dst, tsem.at[n, 0, k], tsem.at[n, 1, k], (me, peer(k)))

    greet([(me, peer(k)) for k in range(1, parts)])
    for k in (2, 1, 3, 0):
        for n in (1, 0):
            tcopy(k, n).start()
    for l in range(layers):
        for i in range(4):
            wcopy(l, i).start()

    lane = lax.broadcasted_iota(jnp.int32, (T, 128), 1)
    first = lane < HD

    def transpose(src, dst, n):
        def body(i, c):
            o = pl.multiple_of(i * 128, 128)
            dst[pl.ds(o, 128), :] = src[:, pl.ds(o, 128)].T
            return c

        lax.fori_loop(0, n // 128, body, 0)

    def rows(fn):
        def body(i, c):
            fn(pl.ds(pl.multiple_of(i * ROW_BLOCK, ROW_BLOCK), ROW_BLOCK))
            return c

        lax.fori_loop(0, T // ROW_BLOCK, body, 0)

    outs = []

    def ship(l, src, dst, k):
        c = pltpu.make_async_copy(src, dst.at[l], osem.at[k])
        c.start()
        outs.append(c)

    for k in range(parts):
        tcopy(k, 1).wait()
    id_rows = [idbuf[k] for k in range(parts)]
    id_cols = jnp.concatenate(
        id_rows + [jnp.zeros((8 - parts, piece), jnp.int32)], axis=0
    ).astype(jnp.float32).T
    for i in range(parts):
        for j in range(parts):
            same = id_cols[:, i : i + 1] == id_rows[j].astype(jnp.float32)
            bias[i * piece : (i + 1) * piece, j * piece : (j + 1) * piece] = jnp.where(same, 0.0, -1e30)
    for k in range(parts):
        tcopy(k, 0).wait()

    for l in range(layers):
        if l == 0:
            hid[...] = low[...].astype(jnp.float32)
        else:
            low[...] = hid[...].astype(jnp.bfloat16)
        for c in outs:
            c.wait()
        outs.clear()
        wcopy(l, 0).wait()
        for k in range(3):
            cols = slice(k * D, (k + 1) * D)
            y = dot(low[...], wq[l, :, cols])
            if k == 0:
                y = (y + b_query[l : l + 1, :]) * 0.125
            if k == 2:
                y = y + b_value[l : l + 1, :]
            qkv[:, cols] = y.astype(jnp.bfloat16)
        ship(l, qkv, o_qkv, 0)
        transpose(low, hidT, D)
        ship(l, hidT, o_hidT, 1)

        def pcopy(i, s):
            return pltpu.make_async_copy(pb.at[s], o_p.at[l, pl.ds(2 * i, 2)], psem.at[s])

        def attend(i, c):
            s = lax.rem(i, 2)
            o = pl.multiple_of(i * 128, 128)
            q2, k2, v2 = (qkv[:, pl.ds(o + k * D, 128)] for k in range(3))

            @pl.when(i >= 2)
            def _():
                pcopy(i - 2, s).wait()

            zero = jnp.zeros_like(q2)
            total = None
            for h in range(2):
                sel = first if h == 0 else ~first
                sc = dot_t(jnp.where(sel, q2, zero), k2) + bias[...]
                e = jnp.exp(sc - jnp.max(sc, axis=-1, keepdims=True))
                p = (e * (1.0 / jnp.sum(e, axis=-1, keepdims=True))).astype(jnp.bfloat16)
                pb[s, h] = p
                part = dot(p, jnp.where(sel, v2, zero))
                total = part if h == 0 else total + part
            pv[:, pl.ds(o, 128)] = total
            mix[:, pl.ds(o, 128)] = total.astype(jnp.bfloat16)
            pcopy(i, s).start()
            return c

        n_pairs = D // 128
        lax.fori_loop(0, n_pairs, attend, 0)
        ship(l, pv, o_pv, 3)
        wcopy(l, 1).wait()
        acc[...] = dot(mix[...], wo[l])
        transpose(mix, mixT, D)
        ship(l, mixT, o_mixT, 4)

        def first_norm(rs):
            x = hid[rs, :] + acc[rs, :] + b_out[l : l + 1, :]
            y, n, r = norm(x, gain_one[l : l + 1, :], shift_one[l : l + 1, :])
            nrm[rs, :] = y
            low[rs, :] = y.astype(jnp.bfloat16)
            n1[rs, :] = n.astype(jnp.bfloat16)
            r1[rs, :] = jnp.broadcast_to(r, (ROW_BLOCK, 128))

        rows(first_norm)
        ship(l, n1, o_n1, 5)
        ship(l, r1, o_r1, 6)
        transpose(low, nrmT, D)
        ship(l, nrmT, o_nrmT, 7)
        wcopy(l, 2).wait()
        wcopy(l, 3).wait()
        acc[...] = nrm[...]

        def ffn(j, c):
            o = pl.multiple_of(j * WIDE, WIDE)
            pre = dot(low[...], wu[l, :, pl.ds(o, WIDE)]) + b_up[l : l + 1, pl.ds(o, WIDE)]
            a, g = gelu_pair(pre)
            al = a.astype(jnp.bfloat16)
            gp[:, pl.ds(o, WIDE)] = g.astype(jnp.bfloat16)
            acc[...] += dot(al, wd[l, pl.ds(o, WIDE), :])
            actT[pl.ds(o, WIDE), :] = al.T
            return c

        lax.fori_loop(0, FF // WIDE, ffn, 0)
        ship(l, gp, o_gp, 8)
        ship(l, actT, o_actT, 9)

        def second_norm(rs):
            x = acc[rs, :] + b_down[l : l + 1, :]
            y, n, r = norm(x, gain_two[l : l + 1, :], shift_two[l : l + 1, :])
            hid[rs, :] = y
            n2[rs, :] = n.astype(jnp.bfloat16)
            r2[rs, :] = jnp.broadcast_to(r, (ROW_BLOCK, 128))

        rows(second_norm)
        ship(l, n2, o_n2, 10)
        ship(l, r2, o_r2, 11)
        for i in (n_pairs - 2, n_pairs - 1):
            pcopy(i, i % 2).wait()

    count = parts * segs
    member_t = jnp.concatenate(
        [
            (lax.broadcasted_iota(jnp.int32, (segs, piece), 0) == row).astype(jnp.float32)
            for row in id_rows
        ],
        axis=1,
    )
    sizes = jnp.sum(member_t, axis=-1, keepdims=True)
    embed = dot(member_t, hid[...], HIGHEST) / sizes
    scale = lax.rsqrt(jnp.sum(embed * embed, axis=-1, keepdims=True) + NORM_EPS)
    unit = embed * scale
    ubuf[...] = jnp.zeros_like(ubuf)
    own = pl.ds(pl.multiple_of(zi * segs, segs), segs)
    gbuf[zi] = unit

    def ucopy(k):
        return remote(gbuf.at[zi], gbuf.at[zi], usem.at[0, k], usem.at[1, k], (me, peer(k)))

    for k in range(1, parts):
        ucopy(k).start()
    for k in range(1, parts):
        ucopy(k).wait()
    for k in range(parts):
        ubuf[k * segs : (k + 1) * segs, :] = gbuf[k]
    units = ubuf[...]
    side = units.shape[0]
    row_no = lax.broadcasted_iota(jnp.int32, (side, side), 0)
    col_no = lax.broadcasted_iota(jnp.int32, (side, side), 1)
    live = (row_no < count) & (col_no < count)
    logits = jnp.where(live, 20.0 * dot_t(units, units, HIGHEST), -1e30)
    top = jnp.max(logits, axis=-1, keepdims=True)
    grown = jnp.exp(logits - top)
    total = jnp.sum(grown, axis=-1, keepdims=True)
    chosen = jnp.where(live & (pair[...] == col_no), 1.0, 0.0)
    picked = jnp.sum(chosen * logits, axis=-1, keepdims=True)
    losses = jnp.where(row_no[:, :1] < count, top + jnp.log(total) - picked, 0.0)
    loss_out[...] = jnp.sum(losses, axis=0, keepdims=True) / count
    pull = jnp.where(live, (grown / total - chosen) * (20.0 * LOSS_SCALE / count), 0.0)
    acc[:side, :side] = pull + pull.T
    grad_unit = dot(acc[own, :side], units, HIGHEST)
    inner = jnp.sum(grad_unit * unit, axis=-1, keepdims=True)
    grad_sums = scale * (grad_unit - unit * inner) / sizes
    for i in range(parts):
        member = (
            lax.broadcasted_iota(jnp.int32, (piece, segs), 1).astype(jnp.float32) == id_cols[:, i : i + 1]
        ).astype(jnp.float32)
        grad_out[i * piece : (i + 1) * piece, :] = dot(member, grad_sums, HIGHEST)
    for c in outs:
        c.wait()


def forward(tokens, segment_ids, pair_ids, w):
    parts, piece, D = tokens.shape
    T = parts * piece
    L = w["w_qkv"].shape[0]
    FF = w["w_up"].shape[2]
    segs = pair_ids.shape[0] // parts
    side = 128
    bf, f32 = jnp.bfloat16, jnp.float32
    S = jax.ShapeDtypeStruct
    V = pltpu.VMEM
    vm = pl.BlockSpec(memory_space=V)
    anyspec = pl.BlockSpec(memory_space=pl.ANY)
    H = D // HD
    dma = pltpu.SemaphoreType.DMA
    out_shape = (
        S((T, D), f32), S((1, 1), f32), S((L, T, 3 * D), bf), S((L, H, T, T), bf), S((L, T, D), f32),
        S((L, D, T), bf), S((L, D, T), bf), S((L, D, T), bf), S((L, FF, T), bf), S((L, T, FF), bf),
        S((L, T, D), bf), S((L, T, 128), f32), S((L, T, D), bf), S((L, T, 128), f32),
    )
    scratch = [
        V((L, D, 3 * D), bf), V((L, D, D), bf), V((L, D, FF), bf), V((L, FF, D), bf),
        V((T, T), f32), V((T, D), f32), V((T, D), bf), V((parts, 1, piece), jnp.int32),
        V((T, 3 * D), bf), V((2, 2, T, T), bf), V((T, D), f32), V((T, D), bf), V((T, D), f32), V((T, FF), bf),
        V((T, D), bf), V((T, 128), f32), V((T, D), bf), V((T, 128), f32),
        V((D, T), bf), V((D, T), bf), V((D, T), bf), V((FF, T), bf), V((T, D), f32),
        V((side, D), f32), V((parts, segs, D), f32),
        dma((L, 4)), dma((2,)), dma((12,)), dma((2, 2, parts)), dma((2, parts)),
    ]
    pair_column = jnp.pad(pair_ids, (0, side - pair_ids.shape[0])).reshape(side, 1)
    return pl.pallas_call(
        functools.partial(fwd_kernel, L, segs),
        out_shape=out_shape,
        in_specs=[anyspec] * 2 + [vm] * 10 + [anyspec] * 4,
        out_specs=(vm, vm) + (anyspec,) * 12,
        scratch_shapes=scratch,
        compiler_params=pltpu.CompilerParams(
            vmem_limit_bytes=60 * 1024 * 1024, collective_id=1, has_side_effects=True
        ),
        name="forward",
    )(
        tokens, segment_ids.reshape(parts, 1, piece), pair_column,
        *(w[k] for k in ("b_query", "b_value", "b_out", "gain_one", "shift_one", "b_up", "b_down", "gain_two", "shift_two")),
        *(w[k] for k in ("w_qkv", "w_out", "w_up", "w_down")),
    )


def low_sum(one, other):
    return (one.astype(jnp.float32) + other.astype(jnp.float32)).astype(jnp.bfloat16)


def bwd_kernel(
    layers, g_in, gain_one, gain_two,
    w_qkv, w_out, w_up, w_down,
    h_qkv, h_p, h_pv, h_hidT, h_mixT, h_nrmT, h_actT, h_gp, h_n1, h_r1, h_n2, h_r2,
    out, gt_out, vec_out,
    wd, wu, gp, actT, wq, qkv, pb, pv, wo, hidT, mixT, nrmT, n1, r1, n2, r2,
    acc, second, branch, gm, gpre, rhs, vec, vrecv, gb,
    sendc, keepq, recvq, s1, k1, t1, s2, k2, t2, za, zr, zb, zt, zf,
    fsem, asem, lsem, csem, xsem, ysem, zsem, osem, vsem, gsem,
):
    T, D = g_in.shape
    FF = w_up.shape[2]
    R = D // WAYS
    U = 4 * R
    n_ffn = FF // D
    n_att = D // 128
    group = D // C
    macros = n_ffn + n_att
    per = n_ffn * group + n_att
    n_units = layers * per
    n_macros = layers * macros

    me = lax.axis_index("dp")
    zi = lax.axis_index("seq")
    oc = lax.rem(me, 2)
    ox = lax.rem(lax.div(me, 2), 2)
    oy = lax.rem(lax.div(me, 4), 2)
    core = (me + 1 - 2 * oc, zi)
    xdev = (me + 2 - 4 * ox, zi)
    ydev = (me + 4 - 8 * oy, zi)
    inner = (zi == 1) | (zi == 2)
    outer = (zi == 0) | (zi == 3)
    to_inner = (me, 1 + lax.div(zi, 2))
    across = (me, 3 - zi)
    to_outer = (me, 3 * lax.div(zi, 2))

    def place(n):
        y = lax.rem(oy + n // 2 % 2, 2)
        x = lax.rem(ox + n % 2, 2)
        return 4 * y + 2 * x + lax.rem(oc + n // 4, 2)

    def turned(src, dst, l):
        return [(src.at[l, place(n)], dst.at[pl.ds(n * R, R)]) for n in range(WAYS)]

    def copies(parts, sem):
        return [pltpu.make_async_copy(a, b, sem.at[k]) for k, (a, b) in enumerate(parts)]

    def ffn_tile(f):
        l = layers - 1 - lax.div(f, n_ffn)
        rb = lax.rem(f, n_ffn)
        s = lax.rem(f, 2)
        span = pl.ds(pl.multiple_of(rb * D, D), D)
        parts = [(w_down.at[l, span], wd.at[s]), (w_up.at[l, :, span], wu.at[s]), (h_gp.at[l, :, span], gp.at[s])]
        parts += [(h_actT.at[l, place(n), rb], actT.at[s, pl.ds(n * R, R)]) for n in range(WAYS)]
        return copies(parts, fsem.at[s])

    def att_tile(a):
        l = layers - 1 - lax.div(a, n_att)
        i = lax.rem(a, n_att)
        s = lax.rem(a, 2)
        parts = [(h_p.at[l, pl.ds(2 * i, 2)], pb.at[s])]
        for k in range(3):
            span = pl.ds(pl.multiple_of(i * 128 + k * D, 128), 128)
            parts.append((w_qkv.at[l, :, span], wq.at[s, :, pl.ds(k * 128, 128)]))
            parts.append((h_qkv.at[l, :, span], qkv.at[s, :, pl.ds(k * 128, 128)]))
        parts.append((h_pv.at[l, :, pl.ds(pl.multiple_of(i * 128, 128), 128)], pv.at[s]))
        return copies(parts, asem.at[s])

    def ffn_layer(l):
        return copies([(h_n2.at[l], n2), (h_r2.at[l], r2)] + turned(h_nrmT, nrmT, l), lsem.at[0])

    def att_layer(l):
        parts = [(h_n1.at[l], n1), (h_r1.at[l], r1), (w_out.at[l], wo)]
        return copies(parts + turned(h_hidT, hidT, l) + turned(h_mixT, mixT, l), lsem.at[1])

    def start(made):
        for c in made:
            c.start()

    def wait(made):
        for c in made:
            c.wait()

    start(ffn_layer(layers - 1))
    for n in range(2):
        start(ffn_tile(jnp.int32(n)))
    start(att_layer(layers - 1))
    for n in range(2):
        start(att_tile(jnp.int32(n)))
    acc[...] = g_in[...]
    vec[...] = jnp.zeros_like(vec)
    greet([core, xdev, ydev] + [(me, lax.rem(zi + k, 4)) for k in range(1, 4)])

    lane = lax.broadcasted_iota(jnp.int32, (T, 128), 1)
    first = lane < HD

    def rows(fn):
        def body(i, sums):
            rs = pl.ds(pl.multiple_of(i * ROW_BLOCK, ROW_BLOCK), ROW_BLOCK)
            return tuple(a + b for a, b in zip(sums, fn(rs)))

        zero = jnp.zeros((1, D), jnp.float32)
        return lax.fori_loop(0, T // ROW_BLOCK, body, (zero, zero, zero))

    def norm_back(g, n, r, gain):
        e = g * gain
        return r * (e - jnp.mean(e, axis=-1, keepdims=True) - n * jnp.mean(e * n, axis=-1, keepdims=True))

    def col_sum(v):
        return jnp.sum(v.astype(jnp.float32), axis=0, keepdims=True)

    def through_norm(normal, root, gain, rounded):
        def fn(rs):
            g = acc[rs, :]
            n = normal[rs, :].astype(jnp.float32)
            d = norm_back(g, n, root[rs, :1], gain)
            acc[rs, :] = d
            low = d.astype(jnp.bfloat16)
            rounded[rs, :] = low
            return col_sum(low), col_sum(g * n), col_sum(g)

        return rows(fn)

    def prologue(l):
        wait(ffn_layer(l))
        sums = through_norm(n2, r2, gain_two[l], second)
        for k in range(3):
            vec[l, 5 + n_ffn + k : 6 + n_ffn + k, :] = sums[k]

    def middle(l):
        wait(att_layer(l))
        sums = through_norm(n1, r1, gain_one[l], branch)
        for k in range(3):
            vec[l, 2 + k : 3 + k, :] = sums[k]
        gm[...] = dot_t(branch[...], wo[...]).astype(jnp.bfloat16)

    def ffn(l, rb, c):
        f = (layers - 1 - l) * n_ffn + rb
        s = lax.rem(f, 2)
        q = rb * group
        wait(ffn_tile(f))
        low = (dot_t(second[...], wd[s]) * gp[s].astype(jnp.float32)).astype(jnp.bfloat16)
        gpre[...] = low
        vec[l, pl.ds(5 + rb, 1), :] = col_sum(low)
        for k, (left, right) in enumerate(((nrmT, gpre), (actT.at[s], second))):
            made = dot(left[...], right[...]).astype(jnp.bfloat16)
            for n in range(group):
                keepq[q + n, k] = made[:U, n * C : (n + 1) * C]
                sendc[c, n, k] = made[U:, n * C : (n + 1) * C]
        acc[...] += dot_t(gpre[...], wu[s])

        @pl.when(f + 2 < layers * n_ffn)
        def _():
            start(ffn_tile(f + 2))

    def attend(l, i, c):
        a = (layers - 1 - l) * n_att + i
        o = pl.multiple_of(i * 128, 128)
        s = lax.rem(a, 2)
        q = n_ffn * group + i
        wait(att_tile(a))
        q2, k2, v2 = (qkv[s, :, k * 128 : (k + 1) * 128] for k in range(3))
        g2 = gm[:, pl.ds(o, 128)]
        weighed = g2.astype(jnp.float32) * pv[s]
        zero = jnp.zeros_like(q2)
        q2t, g2t = q2.T, g2.T
        dq = None
        dkt, dvt = [], []
        for h in range(2):
            sel = first if h == 0 else ~first
            p = pb[s, h]
            gprob = dot_t(jnp.where(sel, g2, zero), v2)
            centre = jnp.sum(jnp.where(sel, weighed, 0.0), axis=-1, keepdims=True)
            ds = (p.astype(jnp.float32) * (gprob - centre)).astype(jnp.bfloat16)
            part = dot(ds, jnp.where(sel, k2, zero))
            dq = part if h == 0 else dq + part
            dkt.append(dot(q2t[h * HD : (h + 1) * HD], ds))
            dvt.append(dot(g2t[h * HD : (h + 1) * HD], p))
        dq = (dq * 0.125).astype(jnp.bfloat16)
        dk = jnp.concatenate(dkt, axis=0).astype(jnp.bfloat16).T
        dv = jnp.concatenate(dvt, axis=0).astype(jnp.bfloat16).T
        vec[l, 0:1, pl.ds(o, 128)] = col_sum(dq)
        vec[l, 1:2, pl.ds(o, 128)] = col_sum(dv)
        rhs[:, :128] = dq
        rhs[:, 128:256] = dk
        rhs[:, 256:] = dv
        made = dot(hidT[...], rhs[...]).astype(jnp.bfloat16)
        keepq[q, 0] = made[:U, :C]
        sendc[c, 0, 0] = made[U:, :C]
        keepq[q, 1, :, :128] = made[:U, C:]
        sendc[c, 0, 1, :, :128] = made[U:, C:]
        made = dot(mixT[...], branch[:, pl.ds(o, 128)]).astype(jnp.bfloat16)
        keepq[q, 1, :, 128:] = made[:U]
        sendc[c, 0, 1, :, 128:] = made[U:]
        acc[...] += dot_t(rhs[...], wq[s])

        @pl.when(a + 2 < layers * n_att)
        def _():
            start(att_tile(a + 2))

    def core_copy(m, wide):
        c = lax.rem(m, 2)
        k = lax.rem(m, macros)
        q = k * group if wide else n_ffn * group + k - n_ffn
        size = group if wide else 1
        return remote(
            sendc.at[c, pl.ds(0, size)], recvq.at[pl.ds(q, size)], csem.at[0, m], csem.at[1, m], core
        )

    def is_wide(m):
        return lax.rem(m, macros) < n_ffn

    def copies_one(u):
        s = lax.rem(u, SLOTS)
        return [
            remote(s1.at[s, k], t1.at[s, k], xsem.at[0, k, s], xsem.at[1, k, s], (xdev, ydev)[k]) for k in range(2)
        ]

    def copies_two(u):
        s = lax.rem(u, SLOTS)
        return [
            remote(s2.at[s, k], t2.at[s, k], ysem.at[0, k, s], ysem.at[1, k, s], (ydev, xdev)[k]) for k in range(2)
        ]

    def copy_in(u):
        s = lax.rem(u, SLOTS)
        return remote(za.at[s], zr.at[s], zsem.at[0, s], zsem.at[1, s], to_inner)

    def copy_across(u):
        s = lax.rem(u, SLOTS)
        return remote(zb.at[s], zt.at[s], zsem.at[2, s], zsem.at[3, s], across)

    def copy_out(u):
        s = lax.rem(u, SLOTS)
        return remote(zf.at[s], out.at[u], zsem.at[4, s], zsem.at[5, s], to_outer)

    def copy_home(u):
        s = lax.rem(u, SLOTS)
        return pltpu.make_async_copy(zf.at[s], out.at[u], osem.at[s])

    def stage_one(u):
        s = lax.rem(u, QUEUE)
        d = lax.rem(u, SLOTS)
        base = lax.div(u, per) * macros

        @pl.when((s < n_ffn * group) & (lax.rem(s, group) == 0))
        def _():
            core_copy(base + lax.div(s, group), True).wait_recv()

        @pl.when(s >= n_ffn * group)
        def _():
            core_copy(base + n_ffn + s - n_ffn * group, False).wait_recv()

        for k in range(2):
            sent, kept = ((1, 3), (0, 2)) if k == 0 else ((2, 3), (0, 1))
            for n, (a, b) in enumerate(zip(sent, kept)):
                to = pl.ds(n * R, R)
                s1[d, k, to] = low_sum(keepq[s, k, pl.ds(a * R, R)], recvq[s, k, pl.ds(a * R, R)])
                k1[d, k, to] = low_sum(keepq[s, k, pl.ds(b * R, R)], recvq[s, k, pl.ds(b * R, R)])
        start(copies_one(u))

    def stage_two(u):
        d = lax.rem(u, SLOTS)
        wait(copies_one(u))
        for k in range(2):
            s2[d, k] = low_sum(k1[d, k, pl.ds(R, R)], t1[d, k, pl.ds(R, R)])
            k2[d, k] = low_sum(k1[d, k, pl.ds(0, R)], t1[d, k, pl.ds(0, R)])
        start(copies_two(u))

    def stage_three(u):
        d = lax.rem(u, SLOTS)
        wait(copies_two(u))
        za[d] = low_sum(k2[d], t2[d])

        @pl.when(outer)
        def _():
            copy_in(u).start()

    def stage_four(u):
        d = lax.rem(u, SLOTS)

        @pl.when(outer)
        def _():
            copy_in(u).wait_send()

        @pl.when(inner)
        def _():
            copy_in(u).wait_recv()
            zb[d] = low_sum(za[d], zr[d])
            copy_across(u).start()

    def stage_five(u):
        d = lax.rem(u, SLOTS)

        @pl.when(inner)
        def _():
            copy_across(u).wait()
            zf[d] = low_sum(zb[d], zt[d])
            copy_out(u).start()
            copy_home(u).start()

    def stage_six(u):
        @pl.when(inner)
        def _():
            copy_out(u).wait_send()
            copy_home(u).wait()

        @pl.when(outer)
        def _():
            copy_out(u).wait_recv()

    stages = (None, stage_one, stage_two, stage_three, stage_four, stage_five, stage_six)

    def run_stage(i, k):
        u = i - LAGS[k]

        @pl.when((u >= 0) & (u < n_units))
        def _():
            stages[k](u)

    def vec_copy(k):
        where = (core, xdev, ydev, to_inner, across, to_outer)[k]
        return remote(vec, vrecv.at[k], vsem.at[0, k], vsem.at[1, k], where)

    def vec_step(k):
        if 1 <= k <= 3:
            vec_copy(k - 1).wait()
            vec[...] += vrecv[k - 1]
        if k < 3:
            vec_copy(k).start()
        if k == 3:

            @pl.when(outer)
            def _():
                vec_copy(3).start()

        if k == 4:

            @pl.when(outer)
            def _():
                vec_copy(3).wait_send()

            @pl.when(inner)
            def _():
                vec_copy(3).wait_recv()
                vec[...] += vrecv[3]
                vec_copy(4).start()

        if k == 5:

            @pl.when(inner)
            def _():
                vec_copy(4).wait()
                vec[...] += vrecv[4]
                vec_copy(5).start()

        if k == 6:

            @pl.when(inner)
            def _():
                vec_copy(5).wait_send()
                vec_out[...] = vec[...]

            @pl.when(outer)
            def _():
                vec_copy(5).wait_recv()
                vec_out[...] = vrecv[5]

    part = T // 4

    def gt_copy(k):
        peer = lax.rem(zi + k, 4)
        src = gb.at[pl.ds(pl.multiple_of(peer * part, part), part)]
        if k == 0:
            return pltpu.make_async_copy(src, gt_out.at[zi], gsem.at[0, 0])
        return remote(src, gt_out.at[zi], gsem.at[0, k], gsem.at[1, k], (me, peer))

    def done_by(i):
        num, den = PACE
        return jnp.minimum(lax.div(num * (i + 1) + den - 1, den), n_macros)

    last = 0
    while -(-PACE[0] * (last + 1) // PACE[1]) < n_macros:
        last += 1

    def step(i, carry):
        for k in range(6, 1, -1):
            run_stage(i, k)
        run_stage(i, 1)
        m = done_by(i - 1)
        l = layers - 1 - lax.div(m, macros)
        k = lax.rem(m, macros)
        c = lax.rem(m, 2)
        busy = done_by(i) > m

        @pl.when(busy & (m >= 2) & is_wide(m - 2))
        def _():
            core_copy(m - 2, True).wait_send()

        @pl.when(busy & (m >= 2) & ~is_wide(m - 2))
        def _():
            core_copy(m - 2, False).wait_send()

        @pl.when(busy & (k == 0))
        def _():
            prologue(l)

        @pl.when(busy & (k == 0) & (l < layers - 1))
        def _():
            start(att_layer(l))

        @pl.when(busy & (k < n_ffn))
        def _():
            ffn(l, k, c)
            core_copy(m, True).start()

        @pl.when(busy & (k == n_ffn) & (l > 0))
        def _():
            start(ffn_layer(l - 1))

        @pl.when(busy & (k == n_ffn))
        def _():
            middle(l)

        @pl.when(busy & (k >= n_ffn))
        def _():
            attend(l, k - n_ffn, c)
            core_copy(m, False).start()

        @pl.when(i == last + 1)
        def _():
            gb[...] = acc[...].astype(jnp.bfloat16)
            for n in range(4):
                gt_copy(n).start()

        for n in range(7):

            @pl.when(i == last + 1 + 2 * n)
            def _(n=n):
                vec_step(n)

        return carry

    lax.fori_loop(0, n_units + LAGS[6], step, 0)
    for m in (n_macros - 2, n_macros - 1):
        core_copy(jnp.int32(m), False).wait_send()
    for n in range(4):
        gt_copy(n).wait()


def backward(grad_hidden, res, w):
    T, D = grad_hidden.shape
    L = w["w_qkv"].shape[0]
    FF = w["w_up"].shape[2]
    bf, f32 = jnp.bfloat16, jnp.float32
    S = jax.ShapeDtypeStruct
    V = pltpu.VMEM
    vm = pl.BlockSpec(memory_space=V)
    anyspec = pl.BlockSpec(memory_space=pl.ANY)
    R = D // WAYS
    U = 4 * R
    group = D // C
    n_units = L * (FF // C + D // 128)
    n_macros = L * (FF // D + D // 128)
    dma = pltpu.SemaphoreType.DMA
    scratch = [
        V((2, D, D), bf), V((2, D, D), bf), V((2, T, D), bf), V((2, D, T), bf),
        V((2, D, 384), bf), V((2, T, 384), bf), V((2, 2, T, T), bf), V((2, T, 128), f32),
        V((D, D), bf), V((D, T), bf), V((D, T), bf), V((D, T), bf),
        V((T, D), bf), V((T, 128), f32), V((T, D), bf), V((T, 128), f32),
        V((T, D), f32), V((T, D), bf), V((T, D), bf), V((T, D), bf), V((T, D), bf), V((T, 384), bf),
        V((L, VEC_ROWS, D), f32), V((6, L, VEC_ROWS, D), f32), V((T, D), bf),
        V((2, group, 2, U, C), bf), V((QUEUE, 2, U, C), bf), V((QUEUE, 2, U, C), bf),
        V((SLOTS, 2, 2 * R, C), bf), V((SLOTS, 2, 2 * R, C), bf), V((SLOTS, 2, 2 * R, C), bf),
        V((SLOTS, 2, R, C), bf), V((SLOTS, 2, R, C), bf), V((SLOTS, 2, R, C), bf),
        V((SLOTS, 2, R, C), bf), V((SLOTS, 2, R, C), bf), V((SLOTS, 2, R, C), bf),
        V((SLOTS, 2, R, C), bf), V((SLOTS, 2, R, C), bf),
        dma((2, 3 + WAYS)), dma((2, 8)), dma((2, 3 + 2 * WAYS)), dma((2, n_macros)), dma((2, 2, SLOTS)), dma((2, 2, SLOTS)),
        dma((6, SLOTS)), dma((SLOTS,)), dma((2, 6)), dma((2, 4)),
    ]
    return pl.pallas_call(
        functools.partial(bwd_kernel, L),
        out_shape=(
            S((n_units, 2, R, C), bf), S((4, T // 4, D), bf), S((L, VEC_ROWS, D), f32),
        ),
        in_specs=[vm] * 3 + [anyspec] * 16,
        out_specs=(anyspec, anyspec, vm),
        scratch_shapes=scratch,
        compiler_params=pltpu.CompilerParams(
            vmem_limit_bytes=60 * 1024 * 1024, collective_id=0, has_side_effects=True
        ),
        name="backward",
    )(
        grad_hidden, w["gain_one"].reshape(L, 1, D), w["gain_two"].reshape(L, 1, D),
        *(w[k] for k in ("w_qkv", "w_out", "w_up", "w_down")),
        *res,
    )


def finish_kernel(units, gt, vec, g_tok, g_qkv, g_out, g_up, g_down, *vectors):
    l = pl.program_id(0)
    R, D = g_out.shape[1:]
    n_ffn = g_up.shape[2] // D
    group = D // C
    g_tok[...] = gt[...].astype(jnp.float32)

    def read(n, k, cols=slice(None)):
        return units[0, n, k, :, cols].astype(jnp.float32)

    for rb in range(n_ffn):
        for n in range(group):
            u = rb * group + n
            g_up[0, :, u * C : (u + 1) * C] = read(u, 0)
            g_down[0, rb * R : (rb + 1) * R, n * C : (n + 1) * C] = read(u, 1)
    for i in range(D // 128):
        u = n_ffn * group + i
        for k in range(3):
            half = slice(k % 2 * 128, k % 2 * 128 + 128)
            g_qkv[0, :, k * D + i * 128 : k * D + (i + 1) * 128] = read(u, k // 2, half)
        g_out[0, :, i * 128 : (i + 1) * 128] = read(u, 1, slice(128, 256))
    row = 0
    for ref in vectors:
        for k in range(ref.shape[1] // D):
            ref[pl.ds(l, 1), k * D : (k + 1) * D] = vec[0, row : row + 1, :]
            row += 1


def finish(units, grad_tokens, vec, layers, hidden_units):
    n_units, _, R, _ = units.shape
    parts, piece, D = grad_tokens.shape
    L, FF = layers, hidden_units
    f32 = jnp.float32
    S = jax.ShapeDtypeStruct
    per = n_units // L
    widths = (D, D, D, D, D, FF, D, D, D)
    return pl.pallas_call(
        finish_kernel,
        grid=(L,),
        out_shape=(
            S((parts, piece, D), f32), S((L, R, 3 * D), f32), S((L, R, D), f32), S((L, R, FF), f32),
            S((L, FF // WAYS, D), f32),
        ) + tuple(S((L, width), f32) for width in widths),
        in_specs=[
            pl.BlockSpec((1, per, 2, R, C), lambda l: (L - 1 - l, 0, 0, 0, 0)),
            pl.BlockSpec((parts // L, piece, D), lambda l: (l, 0, 0)),
            pl.BlockSpec((1, VEC_ROWS, D), lambda l: (l, 0, 0)),
        ],
        out_specs=(
            pl.BlockSpec((parts // L, piece, D), lambda l: (l, 0, 0)),
            pl.BlockSpec((1, R, 3 * D), lambda l: (l, 0, 0)),
            pl.BlockSpec((1, R, D), lambda l: (l, 0, 0)),
            pl.BlockSpec((1, R, FF), lambda l: (l, 0, 0)),
            pl.BlockSpec((1, FF // WAYS, D), lambda l: (l, 0, 0)),
        ) + tuple(pl.BlockSpec((L, width), lambda l: (0, 0)) for width in widths),
        compiler_params=pltpu.CompilerParams(vmem_limit_bytes=48 * 1024 * 1024),
        name="finish",
    )(units.reshape(L, per, 2, R, C), grad_tokens, vec)


NAMES = (
    "w_qkv",
    "b_query",
    "b_value",
    "w_out",
    "b_out",
    "gain_one",
    "shift_one",
    "w_up",
    "b_up",
    "w_down",
    "b_down",
    "gain_two",
    "shift_two",
)


def by_class(array, block, ways):
    layers, rows, tokens_here = array.shape
    if ways == 1:
        return array.reshape(layers, WAYS, -1, tokens_here)
    array = array.reshape(layers, ways, WAYS, block, tokens_here)
    return jnp.swapaxes(array, 1, 2).reshape(layers, WAYS, -1, tokens_here)


def on_device(dp_count, tokens, segment_ids, pair_ids, *weights):
    w = dict(zip(NAMES, weights))
    layer_count, model_width, _ = w["w_qkv"].shape
    hidden_units = w["w_up"].shape[2]
    ways = dp_count // WAYS
    grad_hidden, loss_value, *res = forward(tokens, segment_ids, pair_ids, w)
    for place in (3, 4, 5):
        res[place] = by_class(res[place], model_width // dp_count, ways)
    block = model_width // WAYS
    acts = by_class(res[6], hidden_units // dp_count, ways)
    res[6] = acts.reshape(layer_count, WAYS, -1, block, acts.shape[-1])
    units, grad_tokens, vec = backward(grad_hidden, res, w)
    if ways > 1:
        groups = [[low + WAYS * high for high in range(ways)] for low in range(WAYS)]
        vec = lax.psum(vec, "dp", axis_index_groups=groups)
    grad_tokens, *rest = finish(units, grad_tokens, vec, layer_count, hidden_units)
    matrices, vectors = rest[:4], rest[4:]
    if ways > 1:
        matrices = [
            lax.psum_scatter(
                matrix, "dp", scatter_dimension=1, axis_index_groups=groups, tiled=True
            )
            for matrix in matrices
        ]
    g_qkv, g_out, g_up, g_down = matrices
    return (
        loss_value.reshape(1),
        grad_tokens,
        g_qkv,
        vectors[0],
        vectors[1],
        g_out,
        vectors[2],
        vectors[3],
        vectors[4],
        g_up,
        vectors[5],
        g_down,
        vectors[6],
        vectors[7],
        vectors[8],
    )


def solution(mesh):
    return jax.shard_map(
        functools.partial(on_device, mesh.shape["dp"]),
        mesh=mesh,
        in_specs=(P("dp", "seq", None), P("dp", "seq"), P("dp")) + (P(),) * 13,
        out_specs=(
            P("dp"),
            P("dp", "seq", None),
            P(None, "dp", None),
            P(),
            P(),
            P(None, "dp", None),
            P(),
            P(),
            P(),
            P(None, "dp", None),
            P(),
            P(None, "dp", None),
            P(),
            P(),
            P(),
        ),
        check_vma=False,
    )
```

time: 336 us -> 262 us (0.78)
  blocking collectives: 40.7 us -> 0 us
  local copies, waits for them, and re-layouts: 28.7 us -> 7.99 us
  matrix products: 5.06 us -> 0 us
  other arithmetic: 3.94 us -> 0 us
  starting transfers between devices: 3.5 us -> 0 us
    all_gather x1 -> x0, blocking collectives: 14.7 us -> none  [on_device(): pooled_sums = lax.all_gather(pooled_sums, 'seq', axis=0, tiled=True)]
    unnamed x1 -> x0, blocking collectives: 14.1 us -> none
    all_to_all x1 -> x0, blocking collectives: 11.9 us -> none  [on_device(): row_ids = lax.all_to_all(segment_ids, 'seq', 0, 1, tiled=True)[0]]
    unnamed x41 -> x6, local copies, waits for them, and re-layouts: 11.9 us -> 4.02 us
    convert_element_type x4 -> x0, local copies, waits for them, and re-layouts: 7.48 us -> none  [on_device(): matrix.astype(jnp.float32)]
    dot_general x5 -> x0, matrix products: 5.06 us -> none  [the longest x1 2.04 us: on_device(): pooled_sums = jnp.einsum('ts,td->sd', member, hidden, precision=highest)]
    slice x4 -> x0, local copies, waits for them, and re-layouts: 4.55 us -> none  [the longest x1 1.76 us: on_device(): vec[:, 5 + up_rows + row]]
    all_to_all x1 -> x0, starting transfers between devices: 3.5 us -> none  [on_device(): row_tokens = lax.all_to_all(tokens, 'seq', 0, 1, tiled=True)[0]]
  transfers between devices with their start and end apart: 1 -> 0, of which waited for: 1 -> 0; matrix products, arithmetic and copies ran while one was open for 1% -> 0% of each run, Pallas kernels for 0% -> 0%
where the time goes in v2:
time: 262 us; the launch traced here: 261 us
  Pallas kernels  250 us (95%)
  local copies, waits for them, and re-layouts  7.99 us (3%)
    pallas_call x1, Pallas kernels, backward(): pl.pallas_call(functools.partial(bwd_kernel, L), out_shape=(S((n_units, 2...  156 us
    pallas_call x1, Pallas kernels, forward(): pl.pallas_call(functools.partial(fwd_kernel, L, segs), out_shape=out_shap...  90.4 us

profile of v2, /device:TPU:0, one launch (start us, length us, event | category | flops | bytes accessed | tf_op | source)
XLA Modules:
  0.0 260.5 jit_solution(2860396455150744235)
XLA Ops:
  0.6 0.7 pad_bitcast_fusion
  1.3 1.3 reshape.60.gain_one
  2.6 1.3 reshape.61.gain_two
  3.9 0.7 copy.31.pair
  4.6 90.4 %forward.1 = (f32[512,768]{1,0:T(8,128)}, f32[1,1]{1,0:T(1,128)}, bf16[2,512,2304]{2,1,0:T(8,128)(2,1)}, bf16[2,12,512,512]{3,2,1,0:T(8,128)(2,1)}, f32[2,512,76...) custom-call(bf16[4,128,768]{2,1,0:T(8,128)(2,1)} %tok.1, ...), custom_call_target="tpu_custom_call" | custom-call | tf_op jit(solution)/shard_map/forward/pallas_call | solution.py:341
  95.0 156.2 %backward.1 = (bf16[36,2,96,256]{3,2,1,0:T(8,128)(2,1)}, bf16[4,128,768]{2,1,0:T(8,128)(2,1)}, f32[2,16,768]{2,1,0:T(8,128)}) custom-call(f32[512,768]{1,0:T(8,128)} %get-tuple-element.47.g_in, f32[2,1,768]{2,1,0:T(1,128)} %reshape.60.gain_one, f32[2,1,768]{2,1,0:T(1,128)} %reshape.61.gain_two, bf16[2,768,2304]{2,1,0:T(8,128)(2,1)} %w_qkv.3, ...), custom_call_target="tpu_custom_call" | custom-call | tf_op jit(solution)/shard_map/backward/pallas_call | solution.py:842
  251.2 0.0 copy-start
  251.2 2.0 copy-done
  253.2 0.0 copy-start.1
  253.2 1.1 copy-done.1
  254.3 0.0 copy-start.2
  254.3 0.9 copy-done.2
  255.2 3.6 %finish.1 = (f32[4,128,768]{2,1,0:T(8,128)}, f32[2,96,2304]{2,1,0:T(8,128)}, f32[2,96,768]{2,1,0:T(8,128)}, f32[2,96,3072]{2,1,0:T(8,128)}, f32[2,384,768]{2,1,0...) custom-call(bf16[2,18,2,96,256]{4,3,2,1,0:T(8,128)(2,1)S(1)} %bitcas, ...), custom_call_target="tpu_custom_call" | custom-call | tf_op jit(solution)/shard_map/finish/pallas_call | solution.py:897
Async XLA Ops:
  251.2 2.0 copy-start
  253.2 1.1 copy-start.1
  254.3 0.9 copy-start.2
